TPU v7x, 32 devices: a whole 2x2x4 slice. The times are simulated.
32 devices in a mesh: node: 8 (over z, y), rep: 4 (over x, core).
Axes of the slice: x: 2, y: 2, z: 4, core: 2. Of those that a mesh axis runs over, the one named last changes fastest.
Arguments:
- memory: float32 [8192, 256], P('node'), may hold values from -3 to 3
- hot_memory: float32 [1024, 256], replicated, may hold values from -3 to 3
- cot_cold: float32 [8192, 256], P('node'), may hold values from -6 to 6
- cot_hot: float32 [1024, 256], replicated, may hold values from -6 to 6
- src_local: int32 [32768], P(('node', 'rep')), may hold values from 0 to 1023
- dst_ids: int32 [32768], P(('node', 'rep')), may hold values from 0 to 9215, as said below
- times: int32 [32768], P(('node', 'rep')), may hold values from 0 to 4095
- edge_feat: bfloat16 [32768, 128], P(('node', 'rep')), may hold values from -6 to 6
- cold_list: int32 [256, 128], P(('node', 'rep')), may hold values from 0 to 1023, as said below
- cold_count: int32 [256], P(('node', 'rep')), may hold values from 0 to 128, as said below
- hot_ids: int32 [1024], replicated, may hold values from 8192 to 9215, as said below
- time_freq: float32 [128], replicated, may hold values from 0.001 to 1
- time_phase: float32 [128], replicated, may hold values from -3.140625 to 3.140625
- w_msg: bfloat16 [512, 512], replicated, may hold values from -0.25 to 0.25
- b_msg: float32 [512], replicated, may hold values from -3 to 3
- w_in: bfloat16 [512, 768], replicated, may hold values from -0.25 to 0.25
- w_hid: bfloat16 [256, 768], replicated, may hold values from -0.375 to 0.375
Outputs:
- new_memory: float32 [8192, 256], P('node')
- new_hot: float32 [1024, 256], replicated
- grad_in: float32 [512, 768], replicated
- grad_hid: float32 [256, 768], replicated
Inputs may be any that keep to these rules, and one draw needn't show every extreme that they name: `dst_ids`: each device's events split into cold ones, each named in exactly one used slot of its owner's list, and hot ones whose destination is in hot_ids; cold destinations are node ids below 8192, hot ones 8192 or more. The hot destinations of device d are among the ids 8192 + ((d * 32 + j) mod 1024) for j below 128. `cold_list`: used slots hold distinct event indices of the device; unused slots hold 0. `cold_count`: some owner's list is full on every device. `hot_ids`: A permutation of the hot node ids 8192 to 9215.
All inputs are finite; a program needn't handle non-finite values.
Results may differ from a plain program's by a relative error of at most 0.0018.
The roundings to bfloat16 on the way count: a program that leaves them out, or rounds other values in their place, can miss the bound.
Values may be sent and summed in bfloat16 or wider, within the bound.
A program may use at most 128 MiB of HBM per device.

v0:
```python
import jax
import jax.numpy as jnp
from jax import lax
from jax.sharding import PartitionSpec as P

GRAD_SCALE = 1.0 / 64.0


def gru_forward(agg, mem, w_in, w_hid):
    width = mem.shape[1]
    gate_in = jnp.dot(agg, w_in, preferred_element_type=jnp.float32)
    gate_hid = jnp.dot(mem.astype(jnp.bfloat16), w_hid, preferred_element_type=jnp.float32)
    reset = jax.nn.sigmoid(gate_in[:, :width] + gate_hid[:, :width])
    update = jax.nn.sigmoid(gate_in[:, width : 2 * width] + gate_hid[:, width : 2 * width])
    cand = jnp.tanh(gate_in[:, 2 * width :] + reset * gate_hid[:, 2 * width :])
    fresh = (1.0 - update) * cand + update * mem
    return (fresh, (reset, update, cand, gate_hid[:, 2 * width :]))


def gru_grads(agg, mem, saved, cot):
    reset, update, cand, hid_cand = saved
    d_cand = cot * (1.0 - update) * (1.0 - cand * cand)
    d_upd = cot * (mem - cand) * update * (1.0 - update)
    d_reset = d_cand * hid_cand * reset * (1.0 - reset)
    d_input = jnp.concatenate([d_reset, d_upd, d_cand], axis=1)
    d_hidden = jnp.concatenate([d_reset, d_upd, d_cand * reset], axis=1)
    mem_round = lax.optimization_barrier(mem.astype(jnp.bfloat16)).astype(jnp.float32)
    grad_a = jnp.dot(agg.astype(jnp.float32).T, d_input, precision=lax.Precision.HIGHEST)
    grad_b = jnp.dot(mem_round.T, d_hidden, precision=lax.Precision.HIGHEST)
    return (grad_a, grad_b)


def mean_rows(total, count):
    return (total / jnp.maximum(count, 1.0)[:, None]).astype(jnp.bfloat16)


def forward_rows(total, count, mem, w_in, w_hid):
    agg = mean_rows(total, count)
    fresh, saved = gru_forward(agg, mem, w_in, w_hid)
    live = (count > 0)[:, None]
    return (jnp.where(live, fresh, mem), agg, saved, live)


def on_device(
    memory,
    hot_memory,
    cot_cold,
    cot_hot,
    src_local,
    dst_ids,
    times,
    edge_feat,
    cold_list,
    cold_count,
    hot_ids,
    time_freq,
    time_phase,
    w_msg,
    b_msg,
    w_in,
    w_hid,
):
    n_node = lax.axis_size("node")
    n_rep = lax.axis_size("rep")
    rows_dev = memory.shape[0]
    slot_cap = cold_list.shape[1]
    hot_rows_all = hot_memory.shape[0]
    src_mem = jnp.take(memory, src_local, axis=0).astype(jnp.bfloat16)
    enc = jnp.cos(
        times.astype(jnp.float32)[:, None] * time_freq[None, :] + time_phase[None, :]
    ).astype(jnp.bfloat16)
    raw = jnp.concatenate([src_mem, edge_feat, enc], axis=1)
    messages = jax.nn.silu(
        jnp.dot(raw, w_msg, preferred_element_type=jnp.float32) + b_msg[None, :]
    ).astype(jnp.bfloat16)
    match = (dst_ids[:, None] == hot_ids[None, :]).astype(jnp.bfloat16)
    hot_total = lax.dot_general(
        match, messages, (((0,), (0,)), ((), ())), preferred_element_type=jnp.float32
    )
    hot_cnt = jnp.sum((dst_ids[:, None] == hot_ids[None, :]).astype(jnp.float32), axis=0)
    flat_list = cold_list.reshape(-1)
    slots = jnp.arange(slot_cap, dtype=jnp.int32)
    valid = (slots[None, :] < cold_count[:, None]).reshape(-1)
    owner = jnp.repeat(jnp.arange(n_node, dtype=jnp.int32), slot_cap)
    send_msg = jnp.take(messages, flat_list, axis=0)
    send_row = jnp.where(valid, jnp.take(dst_ids, flat_list) - owner * rows_dev, -1)
    recv_msg, recv_row = (
        lax.all_to_all(send_msg, "node", split_axis=0, concat_axis=0, tiled=True),
        lax.all_to_all(send_row, "node", split_axis=0, concat_axis=0, tiled=True),
    )
    share = rows_dev // n_rep
    first = lax.axis_index("rep") * share
    equal = jnp.arange(rows_dev, dtype=jnp.int32)[:, None] == recv_row[None, :]
    summed = jnp.dot(equal.astype(jnp.bfloat16), recv_msg, preferred_element_type=jnp.float32)
    cold_total, cold_cnt = lax.psum((summed, jnp.sum(equal.astype(jnp.float32), axis=1)), "rep")
    new_memory, agg_cold, saved_cold, live_cold = forward_rows(
        cold_total, cold_cnt, memory, w_in, w_hid
    )
    grad_a, grad_b = gru_grads(
        lax.dynamic_slice_in_dim(agg_cold, first, share, 0),
        lax.dynamic_slice_in_dim(memory, first, share, 0),
        tuple((lax.dynamic_slice_in_dim(item, first, share, 0) for item in saved_cold)),
        jnp.where(
            lax.dynamic_slice_in_dim(live_cold, first, share, 0),
            lax.dynamic_slice_in_dim(cot_cold, first, share, 0),
            0.0,
        ),
    )
    hot_share = hot_rows_all // (n_node * n_rep)
    hot_first = lax.axis_index(("node", "rep")) * hot_share
    hot_total, hot_cnt = lax.psum((hot_total, hot_cnt), ("node", "rep"))
    new_hot, agg_hot, saved_hot, live_hot = forward_rows(
        hot_total, hot_cnt, hot_memory, w_in, w_hid
    )
    hot_a, hot_b = gru_grads(
        lax.dynamic_slice_in_dim(agg_hot, hot_first, hot_share, 0),
        lax.dynamic_slice_in_dim(hot_memory, hot_first, hot_share, 0),
        tuple((lax.dynamic_slice_in_dim(item, hot_first, hot_share, 0) for item in saved_hot)),
        jnp.where(
            lax.dynamic_slice_in_dim(live_hot, hot_first, hot_share, 0),
            lax.dynamic_slice_in_dim(cot_hot, hot_first, hot_share, 0),
            0.0,
        ),
    )
    grad_in, grad_hid = lax.psum((grad_a + hot_a, grad_b + hot_b), ("node", "rep"))
    return (new_memory, new_hot, grad_in * GRAD_SCALE, grad_hid * GRAD_SCALE)


def solution(mesh):
    in_specs = (
        P("node", None),
        P(),
        P("node", None),
        P(),
        P(("node", "rep")),
        P(("node", "rep")),
        P(("node", "rep")),
        P(("node", "rep"), None),
        P(("node", "rep"), None),
        P(("node", "rep")),
        P(),
        P(),
        P(),
        P(),
        P(),
        P(),
        P(),
    )
    out_specs = (P("node", None), P(), P(), P())
    return jax.shard_map(
        on_device, mesh=mesh, in_specs=in_specs, out_specs=out_specs, check_vma=False
    )
```

profile of v0, /device:TPU:1, one launch (start us, length us, event | category | flops | bytes accessed | tf_op | source)
XLA Modules:
  0.0 375.2 jit_solution(4742283008437246685)
XLA Ops:
  8.0 0.0 copy-start
  8.0 0.0 all-reduce.7.cloned.1.call-start
  8.1 0.8 fusion.50
  8.8 0.7 compare_and_fusion
  9.5 0.7 convert_element_type.44
  10.2 0.0 copy-start.16
  10.2 4.8 %gather_fusion.1 = bf16[1024,256]{1,0:T(8,128)(2,1)S(1)} fusion(f32[1024,256]{1,0:T(8,128)} %param.17, s32[1024]{0:T(1024)S(1)} %fusion.50), kind=kCustom, calls=%fused_computation.1 | custom fusion | bytes 1052672 | tf_op jit(solution)/shard_map/jit(_take)/gather | solution.py:68
  15.0 0.2 select_convert_fusion
  15.2 2.0 cosine_convert_fusion
  17.3 0.0 copy-done.14
  17.3 0.0 copy-done.15
  17.3 0.0 copy-done.16
  17.3 0.0 copy-start.1
  17.3 0.0 copy-start.10
  17.3 1.0 multiply_convert_fusion
  18.3 3.0 fusion
  21.3 0.0 all-reduce.7.cloned.1.call-update
  21.3 0.7 copy-done.9
  22.0 0.0 copy-start.13
  22.0 4.5 %gather_fusion = s32[1024]{0:T(1024)S(1)} fusion(s32[1024]{0:T(1024)S(1)} %copy-done.1, s32[1024]{0:T(1024)S(1)} %broadcast_clamp_fusion), kind=kCustom, calls=%fused_computation | custom fusion | bytes 12288 | tf_op jit(solution)/shard_map/jit(_take)/gather | solution.py:86
  26.5 0.7 fusion.47
  27.2 6.4 %all-to-all-start = ((s32[8,128,1]{1,2,0:T(1,128)}), s32[8,128,1]{1,2,0:T(1,128)S(1)}, u32[]{:S(2)}, u32[]{:S(2)}) async-start(s32[8,128,1]{1,2,0:T(1,128)} %bitcast.3), calls=%async_computation | async-start | bytes 8192 | tf_op jit(solution)/shard_map/all_to_all | solution.py:89
  33.6 0.5 fusion.2
  34.1 0.0 copy-start.4
  34.1 0.0 copy-start.7
  34.1 5.1 %gather_fusion.2 = bf16[1024,512]{1,0:T(8,128)(2,1)} fusion(bf16[1024,512]{1,0:T(8,128)(2,1)S(1)} %multiply_convert_fusion, s32[1024]{0:T(1024)S(1)} %broadcast_clamp_fusion), kind=kCustom, calls=%fused_computation.2 | custom fusion | bytes 2101248 | tf_op jit(solution)/shard_map/jit(_take)/gather | solution.py:85
  39.2 40.7 %psum.44 = f32[1024]{0:T(1024)S(1)} all-reduce(f32[1024]{0:T(1024)S(1)} %fusion.2), channel_id=1, replica_groups=mesh['node'=8,'rep'=4] {'node','rep'}, use_global_device_ids=true, to_apply=%region_4.5 | all-reduce | flops 1024 | bytes 8192 | tf_op jit(solution)/shard_map/psum | solution.py:111
  79.9 2.3 fusion.35
  82.2 0.0 copy-done.5
  82.2 1.2 broadcast_select_fusion
  83.4 0.1 dynamic-slice.7
  83.4 0.0 all-to-all-done
  83.4 4.2 %all-to-all-start.1 = ((bf16[8,128,512]{2,1,0:T(8,128)(2,1)}), bf16[8,128,512]{2,1,0:T(8,128)(2,1)}, u32[]{:S(2)}, u32[]{:S(2)}) async-start(bf16[8,128,512]{2,1,0:T(8,128)(2,1)} %broadcast_select_fusion), calls=%async_computation.1 | async-start | bytes 2097152 | tf_op jit(solution)/shard_map/all_to_all | solution.py:88
  87.7 0.0 all-reduce.5.cloned.1.call-start
  87.8 2.2 fusion.37
  90.0 0.5 convert_reduce_fusion
  90.5 7.1 %psum.42 = f32[1024]{0:T(1024)S(1)} all-reduce(f32[1024]{0:T(1024)S(1)} %convert_reduce_fusion), channel_id=1, replica_groups=mesh['node'=8,'rep'=4] {'rep'}, use_global_device_ids=true, to_apply=%region_1.2 | all-reduce | flops 1024 | bytes 8192 | tf_op jit(solution)/shard_map/psum | solution.py:95
  97.7 0.1 dynamic-slice.6
  97.8 61.1 %all-reduce.7.cloned.1.call-done = f32[1024,512]{1,0:T(8,128)} async-done(((f32[1024,512]{1,0:T(8,128)}), f32[1024,512]{1,0:T(8,128)}) %all-reduce.7.cloned.1.call-update) | async-done | bytes 2097168 | tf_op jit(solution)/shard_map/psum | solution.py:111
  158.8 1.8 divide_convert_fusion
  160.6 2.7 fusion.63
  163.3 0.0 all-to-all-done.1
  163.3 3.8 %fusion.3 = f32[1024,512]{1,0:T(8,128)} fusion(bf16[1024,512]{1,0:T(8,128)(2,1)} %bitcast.6, s32[1024]{0:T(1024)S(1)} %bitcast.27), kind=kOutput, calls=%fused_computation.9 | convolution fusion | flops 1074790400 | bytes 3149824 | tf_op jit(solution)/shard_map/dot_general | solution.py:94
  167.1 0.0 all-reduce.5.cloned.1.call-update
  167.1 0.2 all-reduce.9.cloned.1.call-start
  167.4 4.5 %add_select_fusion = (f32[1024,256]{1,0:T(8,128)}, f32[1024,256]{1,0:T(8,128)S(1)}, f32[1024,256]{1,0:T(8,128)S(1)}, f32[1024,256]{1,0:T(8,128)S(1)}, f32[1024,256]{1,0:T(8,128)S(1)}) fusion(f32[1024,256]{1,0:T(8,128)} %param.18, pred[1024]{0:T(1024)(128)(4,1)S(1)} %broadcast_compare_fusion, f32[1024,768]{1,0:T(8,128)} %fusion.35, f32[1024,768]{1,0:T(8,128)} %fusion.63), kind=kLoop, calls=%fused_computation.47 | loop fusion | flops 3932160 | bytes 12583936 | tf_op jit(solution)/shard_map/jit(_where)/select_n | solution.py:41
  171.9 0.9 dynamic-slice_multiply_fusion.1
  172.8 1.4 fusion.42
  174.2 44.0 %all-reduce.5.cloned.1.call-done = f32[1024,512]{1,0:T(8,128)} async-done(((f32[1024,512]{1,0:T(8,128)}), f32[1024,512]{1,0:T(8,128)}) %all-reduce.5.cloned.1.call-update) | async-done | bytes 2097168 | tf_op jit(solution)/shard_map/psum | solution.py:95
  218.1 1.8 divide_convert_fusion.1
  219.9 0.0 copy-start.3
  220.0 1.0 fusion.62
  220.9 0.9 copy-done.3
  221.8 2.1 add_select_fusion.1
  223.9 1.1 dynamic-slice_multiply_fusion
  225.1 0.1 subtract_multiply_fusion
  225.1 0.9 fusion.30
  226.0 0.0 copy-start.6
  226.0 2.0 convolution_add_fusion
  228.0 1.5 convolution_add_fusion.1
  229.5 0.0 all-reduce.9.cloned.1.call-update
  229.5 134.7 %all-reduce.9.cloned.1.call-done = (f32[512,768]{1,0:T(8,128)}, f32[256,768]{1,0:T(8,128)}) async-done(((f32[512,768]{1,0:T(8,128)}, f32[256,768]{1,0:T(8,128)}), (f32[512,768]{1,0:T(8,128)}, f32[256,768]{1,0:T(8,128)})) %all-reduce.9.cloned.1.call-update) | async-done | bytes 2359312 | tf_op jit(solution)/shard_map/psum | solution.py:125
  364.1 2.7 broadcast_multiply_fusion
  366.9 0.9 broadcast_multiply_fusion.1
  (28 shorter events, 0.1 us)
Async XLA Ops:
  8.0 152.6 %copy-start = (bf16[512,768]{1,0:T(8,128)(2,1)S(1)}, bf16[512,768]{1,0:T(8,128)(2,1)}, u32[]{:S(2)}) copy-start(bf16[512,768]{1,0:T(8,128)(2,1)} %param.32) | copy-start | bytes 2359300
  8.0 150.8 %all-reduce.7.cloned.1.call-start = ((), (), s32[]{:S(2)}) async-start(), calls=%async_computation.3 | async-start | bytes 4194304 | tf_op jit(solution)/shard_map/psum | solution.py:111
  10.2 5.0 %copy-start.11 = (f32[128]{0:T(128)S(1)}, f32[128]{0:T(128)}, u32[]{:S(2)}) copy-start(f32[128]{0:T(128)} %param.29) | copy-start | bytes 1540
  10.2 5.0 %copy-start.12 = (f32[128]{0:T(128)S(1)}, f32[128]{0:T(128)}, u32[]{:S(2)}) copy-start(f32[128]{0:T(128)} %param.28) | copy-start | bytes 1540
  10.2 7.1 %copy-start.14 = (bf16[512,512]{1,0:T(8,128)(2,1)S(1)}, bf16[512,512]{1,0:T(8,128)(2,1)}, u32[]{:S(2)}) copy-start(bf16[512,512]{1,0:T(8,128)(2,1)} %param.30) | copy-start | bytes 1572868
  10.2 7.1 %copy-start.15 = (bf16[1024,128]{1,0:T(8,128)(2,1)S(1)}, bf16[1024,128]{1,0:T(8,128)(2,1)}, u32[]{:S(2)}) copy-start(bf16[1024,128]{1,0:T(8,128)(2,1)} %param.24) | copy-start | bytes 786436
  10.2 7.1 %copy-start.16 = (f32[512]{0:T(512)S(1)}, f32[512]{0:T(512)}, u32[]{:S(2)}) copy-start(f32[512]{0:T(512)} %param.31) | copy-start | bytes 6148
  17.3 1.0 copy-start.1
  17.3 1.0 copy-start.10
  21.3 0.7 copy-start.9
  22.0 4.5 %copy-start.13 = (s32[8]{0:T(128)S(1)}, s32[8]{0:T(128)}, u32[]{:S(2)}) copy-start(s32[8]{0:T(128)} %param.26) | copy-start | bytes 100
  27.2 56.2 %all-to-all-start = ((s32[8,128,1]{1,2,0:T(1,128)}), s32[8,128,1]{1,2,0:T(1,128)S(1)}, u32[]{:S(2)}, u32[]{:S(2)}) async-start(s32[8,128,1]{1,2,0:T(1,128)} %bitcast.3), calls=%async_computation | async-start | bytes 8192 | tf_op jit(solution)/shard_map/all_to_all | solution.py:89
  34.1 45.8 %copy-start.4 = (f32[1024,256]{1,0:T(8,128)S(1)}, f32[1024,256]{1,0:T(8,128)}, u32[]{:S(2)}) copy-start(f32[1024,256]{1,0:T(8,128)} %param.18) | copy-start | bytes 3145732
  34.1 45.8 %copy-start.7 = (bf16[256,768]{1,0:T(8,128)(2,1)S(1)}, bf16[256,768]{1,0:T(8,128)(2,1)}, u32[]{:S(2)}) copy-start(bf16[256,768]{1,0:T(8,128)(2,1)} %param.33) | copy-start | bytes 1179652
  79.9 2.3 copy-start.5
  82.2 5.6 %copy-start.2 = (f32[1024,256]{1,0:T(8,128)S(1)}, f32[1024,256]{1,0:T(8,128)}, u32[]{:S(2)}) copy-start(f32[1024,256]{1,0:T(8,128)} %param.17) | copy-start | bytes 3145732
  83.4 79.9 %all-to-all-start.1 = ((bf16[8,128,512]{2,1,0:T(8,128)(2,1)}), bf16[8,128,512]{2,1,0:T(8,128)(2,1)}, u32[]{:S(2)}, u32[]{:S(2)}) async-start(bf16[8,128,512]{2,1,0:T(8,128)(2,1)} %broadcast_select_fusion), calls=%async_computation.1 | async-start | bytes 2097152 | tf_op jit(solution)/shard_map/all_to_all | solution.py:88
  87.7 130.4 %all-reduce.5.cloned.1.call-start = ((), (), s32[]{:S(2)}) async-start(), calls=%async_computation.2 | async-start | bytes 4194304 | tf_op jit(solution)/shard_map/psum | solution.py:95
  167.1 197.0 %all-reduce.9.cloned.1.call-start = ((), (), s32[]{:S(2)}) async-start(), calls=%async_computation.4 | async-start | bytes 4718592 | tf_op jit(solution)/shard_map/psum | solution.py:125
  219.9 1.9 copy-start.3
  226.0 2.0 copy-start.6
  364.1 2.7 copy-start.8
Sparse Core Ops, SparseCore 0:
  21.4 137.3 all-reduce.6
  229.6 134.4 all-reduce.8
Sparse Core Ops, SparseCore 1:
  167.2 50.9 all-reduce.4
where the time goes:
time: 378 us; the launch traced here: 375 us
  waiting for transfers between devices  240 us (63%)
  blocking collectives  47.9 us (13%)
  other arithmetic  23.1 us (6%)
  matrix products  21.6 us (6%)
  local copies, waits for them, and re-layouts  16.2 us (4%)
  between operations  15.8 us (4%)
  starting transfers between devices  10.9 us (3%)
    psum x1, waiting for transfers between devices, on_device(): lax.psum((grad_a + hot_a, grad_b + hot_b), ('node', 'rep'))  135 us
    psum x1, waiting for transfers between devices, on_device(): hot_total, hot_cnt = lax.psum((hot_total, hot_cnt), ('node', 'rep'))  61.1 us
    psum x1, waiting for transfers between devices, on_device(): lax.psum((summed, jnp.sum(equal.astype(jnp.float32), axis=1)), 'rep')  44 us
    psum x1, blocking collectives, on_device(): hot_total, hot_cnt = lax.psum((hot_total, hot_cnt), ('node', 'rep'))  40.7 us
  transfers between devices with their start and end apart: 5, of which 3 were waited for; matrix products, arithmetic and copies ran while one was open for 8% of the time, Pallas kernels for 0%

commit v1 on v0

v1 whole, which is shorter than its diff:
```python
import functools

import jax
import jax.numpy as jnp
from jax import lax
from jax.experimental import pallas as pl
from jax.experimental.pallas import tpu as pltpu
from jax.sharding import PartitionSpec as P

GRAD_SCALE = 1.0 / 64.0
BANDS = 4
MESH = pl.DeviceIdType.MESH
VMEM = pl.BlockSpec(memory_space=pltpu.VMEM)


def greet(devices):
    barrier = pltpu.get_barrier_semaphore()
    for device in devices:
        pl.semaphore_signal(barrier, inc=1, device_id=device, device_id_type=MESH)
    pl.semaphore_wait(barrier, len(devices))


def push(src, dst, send_sem, recv_sem, device):
    copy = pltpu.make_async_remote_copy(
        src_ref=src, dst_ref=dst, send_sem=send_sem, recv_sem=recv_sem, device_id=device, device_id_type=MESH
    )
    copy.start()
    return copy


def exchange_kernel(
    n_node, n_rep,
    msg_ref, rows_ref, hot_ref,
    sum_out, cnt_out, hot_out,
    msg_recv, rows_recv, hot_recv, sums, cnts, core_recv, x_send, x_recv, cnt_core, cnt_send, cnt_x,
    msg_s, msg_r, row_s, row_r, hot_s, hot_r, core_s, core_r, x_s, x_r, cc_s, cc_r, cx_s, cx_r,
):
    nx = n_rep // 2
    n_dev = n_node * n_rep
    node = lax.axis_index("node")
    rep = lax.axis_index("rep")
    core = lax.rem(rep, 2)
    xi = lax.div(rep, 2)
    me = node * n_rep + rep
    cap = msg_ref.shape[1]
    share = sum_out.shape[0]

    def at_node(k):
        return (lax.rem(node + k, n_node), rep)

    def at_linear(k):
        other = lax.rem(me + k, n_dev)
        return (lax.div(other, n_rep), lax.rem(other, n_rep))

    other_core = (node, xi * 2 + 1 - core)

    def at_x(k):
        return (node, lax.rem(xi + k, nx) * 2 + core)

    greet(
        [at_node(k) for k in range(1, n_node)]
        + [other_core]
        + [at_x(k) for k in range(1, nx)]
        + [at_linear(j) for j in range(1, BANDS)]
        + [at_linear(n_dev - j) for j in range(1, BANDS)]
    )

    sent = []
    arrivals = {}
    for k in range(1, n_node):
        other = lax.rem(node + k, n_node)
        row = push(rows_ref.at[other], rows_recv.at[node], row_s.at[k], row_r.at[k], at_node(k))
        msg = push(msg_ref.at[other], msg_recv.at[node], msg_s.at[k], msg_r.at[k], at_node(k))
        arrivals[k] = (row, msg)
        sent += [row, msg]
    hots = [
        push(hot_ref.at[j], hot_recv.at[j - 1], hot_s.at[j - 1], hot_r.at[j - 1], at_linear(j))
        for j in range(1, BANDS)
    ]
    sent += hots

    sums[...] = jnp.zeros_like(sums)
    cnts[...] = jnp.zeros_like(cnts)
    ones = jnp.ones((8, cap), jnp.bfloat16)

    def add_block(rows, block):
        for s in range(n_rep):
            spot = lax.broadcasted_iota(jnp.int32, (share, cap), 0) + s * share
            equal = jnp.where(spot == rows, 1.0, 0.0).astype(jnp.bfloat16)
            sums[s // 2, s % 2] += jnp.dot(equal, block, preferred_element_type=jnp.float32)
            cnts[s] += lax.dot_general(
                ones, equal, (((1,), (1,)), ((), ())), preferred_element_type=jnp.float32
            )

    add_block(rows_ref[node, 0:1, :cap], msg_ref[node])
    for k in range(1, n_node):
        row, msg = arrivals[k]
        row.wait_recv()
        msg.wait_recv()
        origin = lax.rem(node + n_node - k, n_node)
        add_block(rows_recv[origin, 0:1, :cap], msg_recv[origin])

    halves = []
    for k in [*range(1, nx), 0]:
        p = lax.rem(xi + k, nx)
        halves.append((k, p, push(sums.at[p, 1 - core], core_recv.at[k], core_s.at[k], core_r.at[k], other_core)))
    cnt_copy = push(cnts, cnt_core, cc_s, cc_r, other_core)
    sent.append(cnt_copy)
    crossing = []
    for k, p, copy in halves:
        copy.wait_recv()
        sent.append(copy)
        if k:
            x_send[k - 1] = sums[p, core] + core_recv[k]
            crossing.append(push(x_send.at[k - 1], x_recv.at[k - 1], x_s.at[k - 1], x_r.at[k - 1], at_x(k)))
    cnt_copy.wait_recv()
    cnt_send[...] = cnts[...] + cnt_core[...]
    counts = [
        push(cnt_send, cnt_x.at[k - 1], cx_s.at[k - 1], cx_r.at[k - 1], at_x(k)) for k in range(1, nx)
    ]
    for copy in hots:
        copy.wait_recv()
    hot_out[...] = hot_ref[0] + hot_recv[0] + hot_recv[1] + hot_recv[2]
    total = sums[xi, core] + core_recv[0]
    for k, copy in enumerate(crossing):
        copy.wait_recv()
        total += x_recv[k]
    sum_out[...] = total
    number = cnt_send[...]
    for k, copy in enumerate(counts):
        copy.wait_recv()
        number += cnt_x[k]
    cnt_out[...] = number
    for copy in [*sent, *crossing, *counts]:
        copy.wait_send()


def exchange(n_node, n_rep, rows_dev, msg, rows, hot):
    nx = n_rep // 2
    cap, width = msg.shape[1:]
    band, hot_width = hot.shape[1:]
    share = rows_dev // n_rep
    dma = pltpu.SemaphoreType.DMA
    f32 = jnp.float32
    return pl.pallas_call(
        functools.partial(exchange_kernel, n_node, n_rep),
        out_shape=(
            jax.ShapeDtypeStruct((share, width), f32),
            jax.ShapeDtypeStruct((n_rep, 8, share), f32),
            jax.ShapeDtypeStruct((band, hot_width), f32),
        ),
        in_specs=[VMEM] * 3,
        out_specs=(VMEM,) * 3,
        scratch_shapes=[
            pltpu.VMEM(msg.shape, msg.dtype),
            pltpu.VMEM(rows.shape, rows.dtype),
            pltpu.VMEM((BANDS - 1, band, hot_width), f32),
            pltpu.VMEM((nx, 2, share, width), f32),
            pltpu.VMEM((n_rep, 8, share), f32),
            pltpu.VMEM((nx, share, width), f32),
            pltpu.VMEM((nx - 1, share, width), f32),
            pltpu.VMEM((nx - 1, share, width), f32),
            pltpu.VMEM((n_rep, 8, share), f32),
            pltpu.VMEM((n_rep, 8, share), f32),
            pltpu.VMEM((nx - 1, n_rep, 8, share), f32),
            dma((n_node,)), dma((n_node,)), dma((n_node,)), dma((n_node,)),
            dma((BANDS - 1,)), dma((BANDS - 1,)),
            dma((nx,)), dma((nx,)),
            dma((nx - 1,)), dma((nx - 1,)),
            dma, dma,
            dma((nx - 1,)), dma((nx - 1,)),
        ],
        compiler_params=pltpu.CompilerParams(
            collective_id=0, has_side_effects=True, vmem_limit_bytes=40 * 1024 * 1024
        ),
    )(msg, rows, hot)


ORDER_A = ("core", "x", "lo", "hi")
ORDER_B = ("core", "lo", "x", "hi")


def sizes_of(n_node, n_rep):
    return {"core": 2, "x": n_rep // 2, "lo": n_node // 4, "hi": 4}


def finish_kernel(n_node, n_rep, n_sems, ga_ref, gb_ref, cold_ref, hot_ref, oa, ob, ocold, ohot, *scratch):
    sizes = sizes_of(n_node, n_rep)
    recv_a, acc_a, recv_b, acc_b = scratch[0:4], scratch[4:8], scratch[8:12], scratch[12:16]
    send_sem, recv_sem = scratch[16:18]
    node = lax.axis_index("node")
    rep = lax.axis_index("rep")
    nlo = sizes["lo"]
    mine = {"core": lax.rem(rep, 2), "x": lax.div(rep, 2), "lo": lax.rem(node, nlo), "hi": lax.div(node, nlo)}

    def peer(axis, k):
        spot = dict(mine)
        spot[axis] = lax.rem(mine[axis] + k, sizes[axis])
        return (spot["hi"] * nlo + spot["lo"], spot["x"] * 2 + spot["core"])

    greet([peer(axis, k) for axis in ORDER_A for k in range(1, sizes[axis])])

    used = [0]
    everything = []

    def ship(src, dst, device):
        i = used[0]
        used[0] += 1
        copy = push(src, dst, send_sem.at[i], recv_sem.at[i], device)
        everything.append(copy)
        return copy

    def scatter_start(cur, recv, axis):
        size = sizes[axis]
        return [
            ship(cur.at[lax.rem(mine[axis] + k, size)], recv.at[k - 1], peer(axis, k)) for k in range(1, size)
        ]

    def scatter_end(copies, cur, recv, acc, axis):
        total = cur[mine[axis]]
        for k, copy in enumerate(copies):
            copy.wait_recv()
            total = total + recv[k]
        acc[...] = total

    def gather_start(out, order, phase):
        axis = order[phase]
        where = out.at[tuple(mine[a] for a in order[: phase + 1])]
        return [ship(where, where, peer(axis, k)) for k in range(1, sizes[axis])]

    def arrive(copies):
        for copy in copies:
            copy.wait_recv()

    ocold[mine["x"], mine["core"]] = cold_ref[...]
    ohot[tuple(mine[a] for a in ORDER_A)] = hot_ref[...]
    cold_place = ocold.at[mine["x"], mine["core"]]
    first_a = scatter_start(ga_ref, recv_a[0], ORDER_A[0])
    first_b = scatter_start(gb_ref, recv_b[0], ORDER_B[0])
    cold_copies = [ship(cold_place, cold_place, peer("x", k)) for k in range(1, sizes["x"])]
    hot_copies = gather_start(ohot, ORDER_A, 3)

    cur_a, cur_b, copies_a, copies_b = ga_ref, gb_ref, first_a, first_b
    for phase in range(4):
        scatter_end(copies_a, cur_a, recv_a[phase], acc_a[phase], ORDER_A[phase])
        cur_a = acc_a[phase]
        if phase < 3:
            copies_a = scatter_start(cur_a, recv_a[phase + 1], ORDER_A[phase + 1])
        scatter_end(copies_b, cur_b, recv_b[phase], acc_b[phase], ORDER_B[phase])
        cur_b = acc_b[phase]
        if phase < 3:
            copies_b = scatter_start(cur_b, recv_b[phase + 1], ORDER_B[phase + 1])
        if phase == 0:
            arrive(hot_copies)
            hot_copies = gather_start(ohot, ORDER_A, 2)
        if phase == 1:
            arrive(cold_copies)
            side = ocold.at[:, mine["core"]]
            cold_copies = [ship(side, side, peer("core", 1))]
        if phase == 2:
            arrive(hot_copies)
            hot_copies = gather_start(ohot, ORDER_A, 1)
    oa[tuple(mine[a] for a in ORDER_A)] = cur_a[...]
    ob[tuple(mine[a] for a in ORDER_B)] = cur_b[...]
    for phase in (3, 2, 1, 0):
        copies_a = gather_start(oa, ORDER_A, phase)
        copies_b = gather_start(ob, ORDER_B, phase)
        if phase == 2:
            arrive(hot_copies)
            hot_copies = gather_start(ohot, ORDER_A, 0)
        arrive(copies_a)
        arrive(copies_b)
    arrive(hot_copies)
    arrive(cold_copies)
    for copy in everything:
        copy.wait_send()


def finish(n_node, n_rep, ga, gb, cold, hot):
    sizes = sizes_of(n_node, n_rep)
    f32 = jnp.float32
    steps = sum(s - 1 for s in sizes.values())
    n_sems = 4 * steps + sizes["x"] - 1 + 1 + steps
    scratch = []
    for part, order in ((ga, ORDER_A), (gb, ORDER_B)):
        recv, acc = [], []
        for phase in range(4):
            rest = part.shape[phase + 1 :]
            recv.append(pltpu.VMEM((sizes[order[phase]] - 1, *rest), f32))
            acc.append(pltpu.VMEM(rest, f32))
        scratch += recv + acc
    scratch += [pltpu.SemaphoreType.DMA((n_sems,)), pltpu.SemaphoreType.DMA((n_sems,))]
    return pl.pallas_call(
        functools.partial(finish_kernel, n_node, n_rep, n_sems),
        out_shape=(
            jax.ShapeDtypeStruct(ga.shape, f32),
            jax.ShapeDtypeStruct(gb.shape, f32),
            jax.ShapeDtypeStruct((sizes["x"], 2, *cold.shape), f32),
            jax.ShapeDtypeStruct((*(sizes[a] for a in ORDER_A), *hot.shape), f32),
        ),
        in_specs=[VMEM] * 4,
        out_specs=(VMEM,) * 4,
        scratch_shapes=scratch,
        compiler_params=pltpu.CompilerParams(
            collective_id=1, has_side_effects=True, vmem_limit_bytes=40 * 1024 * 1024
        ),
    )(ga, gb, cold, hot)


def on_device(
    memory,
    hot_memory,
    cot_cold,
    cot_hot,
    src_local,
    dst_ids,
    times,
    edge_feat,
    cold_list,
    cold_count,
    hot_ids,
    time_freq,
    time_phase,
    w_msg,
    b_msg,
    w_in,
    w_hid,
):
    f32, bf16 = jnp.float32, jnp.bfloat16
    n_node = lax.axis_size("node")
    n_rep = lax.axis_size("rep")
    n_dev = n_node * n_rep
    rows_dev, width = memory.shape
    slot_cap = cold_list.shape[1]
    hot_rows = hot_memory.shape[0]
    events = src_local.shape[0]
    msg_width = w_msg.shape[1]
    band = hot_rows // n_dev
    share = rows_dev // n_rep
    rep = lax.axis_index("rep")
    me = lax.axis_index("node") * n_rep + rep
    hot_base = n_node * rows_dev

    pick = (src_local[:, None] == jnp.arange(rows_dev, dtype=jnp.int32)[None, :]).astype(bf16)
    src_mem = jnp.dot(pick, memory.astype(bf16), preferred_element_type=f32).astype(bf16)
    enc = jnp.cos(times.astype(f32)[:, None] * time_freq[None, :] + time_phase[None, :]).astype(bf16)
    raw = jnp.concatenate([src_mem, edge_feat, enc], axis=1)
    messages = jax.nn.silu(jnp.dot(raw, w_msg, preferred_element_type=f32) + b_msg[None, :]).astype(bf16)

    local_row = lax.rem(dst_ids, rows_dev)
    lane = jnp.arange(128, dtype=jnp.int32)[None, :]
    extra = jnp.where(
        lane == 0,
        1,
        jnp.where(
            lane == 1,
            lax.div(local_row, 32)[:, None],
            jnp.where(lane == 2, lax.rem(local_row, 32)[:, None], 0),
        ),
    ).astype(bf16)
    wide = jnp.concatenate([messages, extra], axis=1)
    hot_place = jnp.where(
        dst_ids >= hot_base, lax.rem(dst_ids - hot_base + hot_rows - me * band, hot_rows), -1
    )
    flat_list = cold_list.reshape(-1)
    event = jnp.arange(events, dtype=jnp.int32)[None, :]
    listed = (flat_list[:, None] == event).astype(bf16)
    hot_match = (jnp.arange(BANDS * band, dtype=jnp.int32)[:, None] == hot_place[None, :]).astype(bf16)
    sent = jnp.dot(listed, wide, preferred_element_type=f32)
    hot_part = jnp.dot(hot_match, wide, preferred_element_type=f32)
    send_msg = sent[:, :msg_width].astype(bf16).reshape(n_node, slot_cap, msg_width)
    slots = jnp.arange(slot_cap, dtype=jnp.int32)
    valid = slots[None, :] < cold_count[:, None]
    row_at = (sent[:, msg_width + 1] * 32.0 + sent[:, msg_width + 2]).astype(jnp.int32)
    send_row = jnp.where(valid, row_at.reshape(n_node, slot_cap), -1)
    send_row = jnp.pad(send_row, ((0, 0), (0, 128 - slot_cap)), constant_values=-1)
    send_row = jnp.broadcast_to(send_row[:, None, :], (n_node, 8, 128))

    cold_total, cold_cnt, hot_sum = exchange(
        n_node, n_rep, rows_dev, send_msg, send_row, hot_part.reshape(BANDS, band, msg_width + 128)
    )
    first = rep * share
    cold_number = lax.dynamic_index_in_dim(cold_cnt, rep, 0, keepdims=False)[0]
    total = jnp.concatenate([cold_total, hot_sum[:, :msg_width]], axis=0)
    count = jnp.concatenate([cold_number, hot_sum[:, msg_width]], axis=0)

    own_ids = hot_base + me * band + jnp.arange(band, dtype=jnp.int32)
    own = (own_ids[:, None] == hot_ids[None, :]).astype(f32)
    hot_state = jnp.dot(
        own, jnp.concatenate([hot_memory, cot_hot], axis=1), precision=lax.Precision.HIGHEST
    )
    mem = jnp.concatenate([lax.dynamic_slice_in_dim(memory, first, share, 0), hot_state[:, :width]], axis=0)
    cot = jnp.concatenate([lax.dynamic_slice_in_dim(cot_cold, first, share, 0), hot_state[:, width:]], axis=0)

    agg = (total / jnp.maximum(count, 1.0)[:, None]).astype(bf16)
    live = (count > 0)[:, None]
    gate_in = jnp.dot(agg, w_in, preferred_element_type=f32)
    mem_round = mem.astype(bf16)
    gate_hid = jnp.dot(mem_round, w_hid, preferred_element_type=f32)
    reset = jax.nn.sigmoid(gate_in[:, :width] + gate_hid[:, :width])
    update = jax.nn.sigmoid(gate_in[:, width : 2 * width] + gate_hid[:, width : 2 * width])
    hid_cand = gate_hid[:, 2 * width :]
    cand = jnp.tanh(gate_in[:, 2 * width :] + reset * hid_cand)
    fresh = jnp.where(live, (1.0 - update) * cand + update * mem, mem)
    cot = jnp.where(live, cot, 0.0)
    d_cand = cot * (1.0 - update) * (1.0 - cand * cand)
    d_upd = cot * (mem - cand) * update * (1.0 - update)
    d_reset = d_cand * hid_cand * reset * (1.0 - reset)
    d_input = jnp.concatenate([d_reset, d_upd, d_cand], axis=1) * GRAD_SCALE
    d_hidden = jnp.concatenate([d_reset, d_upd, d_cand * reset], axis=1) * GRAD_SCALE
    mem_wide = lax.optimization_barrier(mem_round).astype(f32)
    grad_a = jnp.dot(agg.astype(f32).T, d_input, precision=lax.Precision.HIGHEST)
    grad_b = jnp.dot(mem_wide.T, d_hidden, precision=lax.Precision.HIGHEST)
    grads = jnp.concatenate([grad_a, grad_b], axis=0)
    g_rows, g_cols = grads.shape
    half = g_cols // 2
    sizes = sizes_of(n_node, n_rep)
    piece = g_rows // n_dev
    ga = grads[:, :half].reshape(*(sizes[a] for a in ORDER_A), piece, half)
    gb = grads[:, half:].reshape(*(sizes[a] for a in ORDER_B), piece, half)
    oa, ob, new_cold, hot_blocks = finish(n_node, n_rep, ga, gb, fresh[:share], fresh[share:])
    grads = jnp.concatenate([oa.reshape(g_rows, half), ob.reshape(g_rows, half)], axis=1)
    agg_rows = w_in.shape[0]

    ids = hot_ids - hot_base
    block, inner = lax.div(ids, band), lax.rem(ids, band)
    at_node, at_rep = lax.div(block, n_rep), lax.rem(block, n_rep)
    hi, lo = lax.div(at_node, sizes["lo"]), lax.rem(at_node, sizes["lo"])
    xi, core = lax.div(at_rep, 2), lax.rem(at_rep, 2)
    place = (((core * sizes["x"] + xi) * sizes["lo"] + lo) * sizes["hi"] + hi) * band + inner
    new_hot = jnp.take(hot_blocks.reshape(hot_rows, width), place, axis=0)
    return (new_cold.reshape(rows_dev, width), new_hot, grads[:agg_rows], grads[agg_rows:])


def solution(mesh):
    both = P(("node", "rep"))
    in_specs = (
        P("node", None),
        P(),
        P("node", None),
        P(),
        both,
        both,
        both,
        P(("node", "rep"), None),
        P(("node", "rep"), None),
        both,
        P(),
        P(),
        P(),
        P(),
        P(),
        P(),
        P(),
    )
    out_specs = (P("node", None), P(), P(), P())
    return jax.shard_map(on_device, mesh=mesh, in_specs=in_specs, out_specs=out_specs, check_vma=False)
```

time: 378 us -> 134 us (0.35)
  waiting for transfers between devices: 240 us -> 0 us
  Pallas kernels: 0 us -> 98.1 us
  blocking collectives: 47.9 us -> 0 us
  between operations: 15.8 us -> 1.03 us
  other arithmetic: 23.1 us -> 9.41 us
  matrix products: 21.6 us -> 10.7 us
  starting transfers between devices: 10.9 us -> 0 us
    psum x3 -> x0, waiting for transfers between devices: 240 us -> none  [the longest x1 135 us: on_device(): lax.psum((grad_a + hot_a, grad_b + hot_b), ('node', 'rep'))]
    pallas_call x0 -> x2, Pallas kernels: none -> 98.1 us  [the longest x1 57.5 us: finish(): pl.pallas_call(functools.partial(finish_kernel, n_node, n_rep, n_sems), o...]
    psum x2 -> x0, blocking collectives: 47.9 us -> none  [the longest x1 40.7 us: on_device(): hot_total, hot_cnt = lax.psum((hot_total, hot_cnt), ('node', 'rep'))]
    dot_general x11 -> x9, matrix products: 21.6 us -> 10.7 us  [the longest x1 2.15 us: on_device(): jnp.dot(own, jnp.concatenate([hot_memory, cot_hot], axis=1), precision=la...]
    all_to_all x2 -> x0, starting transfers between devices: 10.6 us -> none  [the longest x1 6.38 us: on_device(): lax.all_to_all(send_row, 'node', split_axis=0, concat_axis=0, tiled=True)]
    gather x3 -> x1, local copies, waits for them, and re-layouts: 14.4 us -> 4.68 us  [on_device(): new_hot = jnp.take(hot_blocks.reshape(hot_rows, width), place, axis=0)]
    mul x6 -> x2, other arithmetic: 5.72 us -> 0.37 us  [the longest x1 0.27 us: on_device(): d_cand * reset]
    select_n x5 -> x4, other arithmetic: 8.46 us -> 3.52 us  [the longest x1 2.4 us: on_device(): new_hot = jnp.take(hot_blocks.reshape(hot_rows, width), place, axis=0)]
  transfers between devices with their start and end apart: 5 -> 0, of which waited for: 3 -> 0; matrix products, arithmetic and copies ran while one was open for 8% -> 0% of each run, Pallas kernels for 0% -> 0%
where the time goes in v1:
time: 134 us; the launch traced here: 132 us
  Pallas kernels  98.1 us (73%)
  local copies, waits for them, and re-layouts  13.1 us (10%)
  matrix products  10.7 us (8%)
  other arithmetic  9.41 us (7%)
    pallas_call x1, Pallas kernels, finish(): pl.pallas_call(functools.partial(finish_kernel, n_node, n_rep, n_sems), o...  57.5 us
    pallas_call x1, Pallas kernels, exchange(): pl.pallas_call(functools.partial(exchange_kernel, n_node, n_rep), out_sha...  40.6 us
    gather x1, local copies, waits for them, and re-layouts, on_device(): new_hot = jnp.take(hot_blocks.reshape(hot_rows, width), place, axis=0)  4.68 us
    unnamed x33, local copies, waits for them, and re-layouts  3.66 us
    slice x2, local copies, waits for them, and re-layouts, on_device(): sent[:, :msg_width].astype(bf16).reshape(n_node, slot_cap, msg_width)  2.8 us

profile of v1, /device:TPU:1, one launch (start us, length us, event | category | flops | bytes accessed | tf_op | source)
XLA Modules:
  0.0 132.3 jit_solution(7902518746024686544)
XLA Ops:
  0.6 0.0 copy-start
  0.6 0.0 copy-start.8
  0.7 0.0 copy-start.10
  0.7 0.0 copy-start.9
  0.7 0.0 copy-start.13
  0.7 0.0 copy-start.12
  0.7 0.0 copy-start.15
  0.7 0.8 fusion.41
  1.5 0.2 select_convert_fusion
  1.7 2.1 %fusion.9 = bf16[1024,256]{1,0:T(8,128)(2,1)S(1)} fusion(s32[1024]{0:T(1024)} %param.21, f32[1024,256]{1,0:T(8,128)} %param.17), kind=kOutput, calls=%fused_computation.19 | convolution fusion | flops 538443776 | bytes 1576960 | tf_op jit(solution)/shard_map/dot_general | solution.py:345
  3.8 0.0 copy-done.8
  3.9 0.0 copy-done.10
  3.9 0.0 copy-done.9
  3.9 2.0 %cosine_convert_fusion = bf16[1024,128]{1,0:T(8,128)(2,1)S(1)} fusion(f32[128]{0:T(128)S(1)} %copy-done.9, f32[128]{0:T(128)S(1)} %copy-done.10, f32[1024]{0:T(1024)S(1)} %convert_element_type.44), kind=kLoop, calls=%fused_computation.41 | loop fusion | flops 393216 | bytes 267264 | tf_op jit(solution)/shard_map/convert_element_type | solution.py:346
  5.9 0.0 copy-done.13
  5.9 0.0 copy-done.12
  5.9 0.0 copy-done.15
  5.9 1.0 multiply_convert_fusion
  7.0 0.0 copy-start.14
  7.0 0.5 fusion.20
  7.6 0.1 copy-done.14
  7.7 1.7 %fusion = f32[1024,640]{0,1:T(8,128)S(1)} fusion(s32[1024]{0:T(1024)S(1)} %bitcast.29, bf16[1024,128]{0,1:T(8,128)(2,1)S(1)} %select_convert_fusion, bf16[1024,512]{0,1:T(8,128)(2,1)S(1)} %multiply_convert_fusion), kind=kOutput, calls=%fused_computation.3 | convolution fusion | flops 1345847296 | bytes 3936256 | tf_op jit(solution)/shard_map/dot_general | solution.py:369
  9.4 0.0 copy-start.3
  9.4 1.5 %copy-done.3 = f32[1024,640]{0,1:T(8,128)} copy-done((f32[1024,640]{0,1:T(8,128)}, f32[1024,640]{0,1:T(8,128)S(1)}, u32[]{:S(2)}) %copy-start.3) | copy-done | bytes 2621464
  10.9 0.0 copy-start.11
  10.9 1.1 slice.170
  12.0 1.7 %copy.22 = bf16[1024,512]{1,0:T(8,128)(2,1)S(1)} copy(bf16[1024,512]{0,1:T(8,128)(2,1)} %slice.170) | data formatting | bytes 2097152 | tf_op jit(solution)/shard_map/slice | solution.py:371
  13.7 0.8 fusion.50
  14.6 0.0 copy-done.11
  14.6 0.1 fusion.53
  14.7 40.6 %shard_map.192 = (f32[256,512]{1,0:T(8,128)S(1)}, f32[4,8,256]{2,1,0:T(8,128)S(1)}, f32[32,640]{1,0:T(8,128)S(1)}) custom-call(bf16[8,128,512]{2,1,0:T(8,128)(2,1)S(1)} %bitcast.23, s32[8,8,128]{2,1,0:T(8,128)S(1)} %broadcast_in_dim.118.rows_ref, f32[4,32,640]{2,1,0:T(8,128)S(1)} %bitcast.25), custom_call_target="tpu_custom_call" | custom-call | tf_op jit(solution)/shard_map/pallas_call | solution.py:145
  55.2 0.1 slice_reduce_fusion
  55.4 0.0 copy-start.5
  55.4 0.0 copy-done
  55.4 0.0 copy-start.1
  55.4 0.0 copy-start.7
  55.4 0.4 fusion.65
  55.9 0.1 copy-done.5
  56.0 1.8 %constant_dynamic-slice_fusion = (f32[256,256]{1,0:T(8,128)S(1)}, f32[256,256]{1,0:T(8,128)}) fusion(f32[1024,256]{1,0:T(8,128)} %param.17, s32[]{:T(128)S(6)} %select_n.55, f32[1024,256]{1,0:T(8,128)} %param.19), kind=kLoop, calls=%fused_computation.112 | loop fusion | bytes 1048580 | tf_op jit(solution)/shard_map/dynamic_slice | solution.py:392
  57.8 0.0 copy-start.4
  57.8 0.0 copy-done.1
  57.8 0.0 copy-done.7
  57.8 2.2 %fusion.2 = f32[32,512]{1,0:T(8,128)S(1)} fusion(f32[1024,256]{1,0:T(8,128)S(1)} %copy-done.1, f32[1024,256]{1,0:T(8,128)} %param.18, s32[1024]{0:T(1024)S(1)} %copy-done.7, s32[32]{0:T(128)S(1)} %iota_add_fusion), kind=kOutput, calls=%fused_computation.10 | convolution fusion | flops 201883648 | bytes 2166912 | tf_op jit(solution)/shard_map/dot_general | solution.py:389
  60.0 0.0 copy-done.4
  60.0 0.0 copy-start.2
  60.0 0.3 fusion.70
  60.3 0.2 add_select_fusion
  60.6 0.4 copy-done.2
  61.0 0.0 copy-start.6
  61.0 0.3 fusion.67
  61.2 0.1 subtract_multiply_fusion
  61.4 0.5 copy-done.6
  61.8 1.5 %fusion.16 = f32[512,768]{1,0:T(8,128)S(1)} fusion(f32[288,256]{1,0:T(8,128)S(1)} %get-tuple-element.23, f32[288,256]{1,0:T(8,128)S(1)} %get-tuple-element.24, f32[288,256]{1,0:T(8,128)S(1)} %subtract_multiply_fusion, f32[32,512]{1,0:T(8,128)S(1)} %copy-done.6, f32[256,512]{1,0:T(8,128)S(1)} %get-tuple-element.11, f32[288]{0:T(512)S(1)} %fusion.55), kind=kOutput, calls=%fused_computation.28 | convolution fusion | flops 1360060416 | bytes 3048576 | tf_op jit(solution)/shard_map/dot_general | solution.py:412
  63.4 0.9 fusion.18
  64.3 0.2 pad_maximum_fusion.1
  64.5 57.5 %shard_map.193 = (f32[2,2,2,4,24,384]{5,4,3,2,1,0:T(8,128)S(1)}, f32[2,2,2,4,24,384]{5,4,3,2,1,0:T(8,128)S(1)}, f32[2,2,256,256]{3,2,1,0:T(8,128)S(1)}, f32[2,2,2,4,32,256]{5,4,3,2,1,0:T(8,128)S(1)}) custom-call(f32[2,2,2,4,24,384]{5,4,3,2,1,0:T(8,128)S(1)} %bitcast.22, f32[2,2,2,4,24,384]{5,4,3,2,1,0:T(8,128)S(1)} %bitcast.21, ...), custom_call_target="tpu_custom_call" | custom-call | tf_op jit(solution)/shard_map/pallas_call | solution.py:293
  122.0 0.9 pad_maximum_fusion.7
  122.9 1.3 fusion.8
  124.2 4.7 %gather_fusion = f32[1024,256]{1,0:T(8,128)} fusion(f32[1024,256]{1,0:T(8,128)S(1)} %bitcast.16, s32[1024]{0:T(1024)S(1)} %broadcast_clamp_fusion), kind=kCustom, calls=%fused_computation | custom fusion | bytes 2101248 | tf_op jit(solution)/shard_map/jit(_take)/gather | solution.py:431
  128.9 2.4 %broadcast_select_fusion = f32[1024,256]{1,0:T(8,128)} fusion(f32[1024,256]{1,0:T(8,128)} %gather_fusion, pred[1024]{0:T(1024)(128)(4,1)S(1)} %get-tuple-element.18), kind=kLoop, calls=%fused_computation.38 | loop fusion | flops 262144 | bytes 2098176 | tf_op jit(solution)/shard_map/jit(_take)/select_n | solution.py:431
  131.3 1.0 copy.24
  (15 shorter events, 0.1 us)
Async XLA Ops:
  0.6 54.8 %copy-start = (bf16[512,768]{1,0:T(8,128)(2,1)S(1)}, bf16[512,768]{1,0:T(8,128)(2,1)}, u32[]{:S(2)}) copy-start(bf16[512,768]{1,0:T(8,128)(2,1)} %param.32) | copy-start | bytes 2359300
  0.6 3.2 %copy-start.8 = (s32[1024]{0:T(1024)S(1)}, s32[1024]{0:T(1024)}, u32[]{:S(2)}) copy-start(s32[1024]{0:T(1024)} %param.23) | copy-start | bytes 12292
  0.7 3.2 %copy-start.10 = (f32[128]{0:T(128)S(1)}, f32[128]{0:T(128)}, u32[]{:S(2)}) copy-start(f32[128]{0:T(128)} %param.28) | copy-start | bytes 1540
  0.7 3.2 %copy-start.9 = (f32[128]{0:T(128)S(1)}, f32[128]{0:T(128)}, u32[]{:S(2)}) copy-start(f32[128]{0:T(128)} %param.29) | copy-start | bytes 1540
  0.7 5.2 %copy-start.13 = (bf16[1024,128]{1,0:T(8,128)(2,1)S(1)}, bf16[1024,128]{1,0:T(8,128)(2,1)}, u32[]{:S(2)}) copy-start(bf16[1024,128]{1,0:T(8,128)(2,1)} %param.24) | copy-start | bytes 786436
  0.7 5.2 %copy-start.12 = (bf16[512,512]{1,0:T(8,128)(2,1)S(1)}, bf16[512,512]{1,0:T(8,128)(2,1)}, u32[]{:S(2)}) copy-start(bf16[512,512]{1,0:T(8,128)(2,1)} %param.30) | copy-start | bytes 1572868
  0.7 5.2 %copy-start.15 = (f32[512]{0:T(512)S(1)}, f32[512]{0:T(512)}, u32[]{:S(2)}) copy-start(f32[512]{0:T(512)} %param.31) | copy-start | bytes 6148
  7.0 0.7 copy-start.14
  9.4 1.5 %copy-start.3 = (f32[1024,640]{0,1:T(8,128)}, f32[1024,640]{0,1:T(8,128)S(1)}, u32[]{:S(2)}) copy-start(f32[1024,640]{0,1:T(8,128)S(1)} %fusion) | copy-start | bytes 7864324
  10.9 3.7 %copy-start.11 = (s32[8]{0:T(128)S(1)}, s32[8]{0:T(128)}, u32[]{:S(2)}) copy-start(s32[8]{0:T(128)} %param.26) | copy-start | bytes 100
  55.4 0.6 copy-start.5
  55.4 2.4 %copy-start.1 = (f32[1024,256]{1,0:T(8,128)S(1)}, f32[1024,256]{1,0:T(8,128)}, u32[]{:S(2)}) copy-start(f32[1024,256]{1,0:T(8,128)} %param.20) | copy-start | bytes 3145732
  55.4 2.4 %copy-start.7 = (s32[1024]{0:T(1024)S(1)}, s32[1024]{0:T(1024)}, u32[]{:S(2)}) copy-start(s32[1024]{0:T(1024)} %param.27) | copy-start | bytes 12292
  57.8 2.2 %copy-start.4 = (bf16[256,768]{1,0:T(8,128)(2,1)S(1)}, bf16[256,768]{1,0:T(8,128)(2,1)}, u32[]{:S(2)}) copy-start(bf16[256,768]{1,0:T(8,128)(2,1)} %param.33) | copy-start | bytes 1179652
  60.0 1.0 copy-start.2
  61.0 0.8 copy-start.6

commit v2 on v1

--- a/solution.py
+++ b/solution.py
@@ -30,9 +30,9 @@
 
 def exchange_kernel(
     n_node, n_rep,
-    msg_ref, rows_ref, hot_ref,
+    msg0_ref, msg1_ref, rows_ref, hot_ref,
     sum_out, cnt_out, hot_out,
-    msg_recv, rows_recv, hot_recv, sums, cnts, core_recv, x_send, x_recv, cnt_core, cnt_send, cnt_x,
+    recv0, recv1, rows_recv, hot_recv, sums, cnts, core_recv, x_send, x_recv, cnt_core, cnt_send, cnt_x,
     msg_s, msg_r, row_s, row_r, hot_s, hot_r, core_s, core_r, x_s, x_r, cc_s, cc_r, cx_s, cx_r,
 ):
     nx = n_rep // 2
@@ -42,7 +42,7 @@
     core = lax.rem(rep, 2)
     xi = lax.div(rep, 2)
     me = node * n_rep + rep
-    cap = msg_ref.shape[1]
+    cap, part = msg0_ref.shape[1:]
     share = sum_out.shape[0]
 
     def at_node(k):
@@ -69,10 +69,12 @@
     arrivals = {}
     for k in range(1, n_node):
         other = lax.rem(node + k, n_node)
-        row = push(rows_ref.at[other], rows_recv.at[node], row_s.at[k], row_r.at[k], at_node(k))
-        msg = push(msg_ref.at[other], msg_recv.at[node], msg_s.at[k], msg_r.at[k], at_node(k))
-        arrivals[k] = (row, msg)
-        sent += [row, msg]
+        arrivals["row", k] = push(rows_ref.at[other], rows_recv.at[node], row_s.at[k], row_r.at[k], at_node(k))
+    for h, (src, dst) in enumerate(((msg0_ref, recv0), (msg1_ref, recv1))):
+        for k in range(1, n_node):
+            other = lax.rem(node + k, n_node)
+            arrivals[h, k] = push(src.at[other], dst.at[node], msg_s.at[h, k], msg_r.at[h, k], at_node(k))
+    sent += list(arrivals.values())
     hots = [
         push(hot_ref.at[j], hot_recv.at[j - 1], hot_s.at[j - 1], hot_r.at[j - 1], at_linear(j))
         for j in range(1, BANDS)
@@ -83,61 +85,69 @@
     cnts[...] = jnp.zeros_like(cnts)
     ones = jnp.ones((8, cap), jnp.bfloat16)
 
-    def add_block(rows, block):
+    def add_block(h, rows, block):
         for s in range(n_rep):
             spot = lax.broadcasted_iota(jnp.int32, (share, cap), 0) + s * share
             equal = jnp.where(spot == rows, 1.0, 0.0).astype(jnp.bfloat16)
-            sums[s // 2, s % 2] += jnp.dot(equal, block, preferred_element_type=jnp.float32)
-            cnts[s] += lax.dot_general(
-                ones, equal, (((1,), (1,)), ((), ())), preferred_element_type=jnp.float32
-            )
-
-    add_block(rows_ref[node, 0:1, :cap], msg_ref[node])
-    for k in range(1, n_node):
-        row, msg = arrivals[k]
-        row.wait_recv()
-        msg.wait_recv()
-        origin = lax.rem(node + n_node - k, n_node)
-        add_block(rows_recv[origin, 0:1, :cap], msg_recv[origin])
-
-    halves = []
-    for k in [*range(1, nx), 0]:
-        p = lax.rem(xi + k, nx)
-        halves.append((k, p, push(sums.at[p, 1 - core], core_recv.at[k], core_s.at[k], core_r.at[k], other_core)))
-    cnt_copy = push(cnts, cnt_core, cc_s, cc_r, other_core)
-    sent.append(cnt_copy)
-    crossing = []
-    for k, p, copy in halves:
-        copy.wait_recv()
-        sent.append(copy)
-        if k:
-            x_send[k - 1] = sums[p, core] + core_recv[k]
-            crossing.append(push(x_send.at[k - 1], x_recv.at[k - 1], x_s.at[k - 1], x_r.at[k - 1], at_x(k)))
-    cnt_copy.wait_recv()
-    cnt_send[...] = cnts[...] + cnt_core[...]
-    counts = [
-        push(cnt_send, cnt_x.at[k - 1], cx_s.at[k - 1], cx_r.at[k - 1], at_x(k)) for k in range(1, nx)
-    ]
+            sums[h, s // 2, s % 2] += jnp.dot(equal, block, preferred_element_type=jnp.float32)
+            if h == 0:
+                cnts[s] += lax.dot_general(
+                    ones, equal, (((1,), (1,)), ((), ())), preferred_element_type=jnp.float32
+                )
+
+    crossing = [[], []]
+    counts = []
+    for h, (mine, got) in enumerate(((msg0_ref, recv0), (msg1_ref, recv1))):
+        add_block(h, rows_ref[node, 0:1, :cap], mine[node])
+        for k in range(1, n_node):
+            if h == 0:
+                arrivals["row", k].wait_recv()
+            arrivals[h, k].wait_recv()
+            origin = lax.rem(node + n_node - k, n_node)
+            add_block(h, rows_recv[origin, 0:1, :cap], got[origin])
+        halves = []
+        for k in [*range(1, nx), 0]:
+            p = lax.rem(xi + k, nx)
+            copy = push(sums.at[h, p, 1 - core], core_recv.at[h, k], core_s.at[h, k], core_r.at[h, k], other_core)
+            halves.append((k, p, copy))
+        if h == 0:
+            cnt_copy = push(cnts, cnt_core, cc_s, cc_r, other_core)
+            sent.append(cnt_copy)
+        for k, p, copy in halves:
+            copy.wait_recv()
+            sent.append(copy)
+            if k:
+                x_send[h, k - 1] = sums[h, p, core] + core_recv[h, k]
+                crossing[h].append(
+                    push(x_send.at[h, k - 1], x_recv.at[h, k - 1], x_s.at[h, k - 1], x_r.at[h, k - 1], at_x(k))
+                )
+        if h == 0:
+            cnt_copy.wait_recv()
+            cnt_send[...] = cnts[...] + cnt_core[...]
+            counts = [
+                push(cnt_send, cnt_x.at[k - 1], cx_s.at[k - 1], cx_r.at[k - 1], at_x(k)) for k in range(1, nx)
+            ]
     for copy in hots:
         copy.wait_recv()
     hot_out[...] = hot_ref[0] + hot_recv[0] + hot_recv[1] + hot_recv[2]
-    total = sums[xi, core] + core_recv[0]
-    for k, copy in enumerate(crossing):
-        copy.wait_recv()
-        total += x_recv[k]
-    sum_out[...] = total
     number = cnt_send[...]
     for k, copy in enumerate(counts):
         copy.wait_recv()
         number += cnt_x[k]
     cnt_out[...] = number
-    for copy in [*sent, *crossing, *counts]:
+    for h in range(2):
+        total = sums[h, xi, core] + core_recv[h, 0]
+        for k, copy in enumerate(crossing[h]):
+            copy.wait_recv()
+            total += x_recv[h, k]
+        sum_out[:, h * part : (h + 1) * part] = total
+    for copy in [*sent, *crossing[0], *crossing[1], *counts]:
         copy.wait_send()
 
 
-def exchange(n_node, n_rep, rows_dev, msg, rows, hot):
+def exchange(n_node, n_rep, rows_dev, msg0, msg1, rows, hot):
     nx = n_rep // 2
-    cap, width = msg.shape[1:]
+    part = msg0.shape[2]
     band, hot_width = hot.shape[1:]
     share = rows_dev // n_rep
     dma = pltpu.SemaphoreType.DMA
@@ -145,35 +155,36 @@
     return pl.pallas_call(
         functools.partial(exchange_kernel, n_node, n_rep),
         out_shape=(
-            jax.ShapeDtypeStruct((share, width), f32),
+            jax.ShapeDtypeStruct((share, 2 * part), f32),
             jax.ShapeDtypeStruct((n_rep, 8, share), f32),
             jax.ShapeDtypeStruct((band, hot_width), f32),
         ),
-        in_specs=[VMEM] * 3,
+        in_specs=[VMEM] * 4,
         out_specs=(VMEM,) * 3,
         scratch_shapes=[
-            pltpu.VMEM(msg.shape, msg.dtype),
+            pltpu.VMEM(msg0.shape, msg0.dtype),
+            pltpu.VMEM(msg1.shape, msg1.dtype),
             pltpu.VMEM(rows.shape, rows.dtype),
             pltpu.VMEM((BANDS - 1, band, hot_width), f32),
-            pltpu.VMEM((nx, 2, share, width), f32),
+            pltpu.VMEM((2, nx, 2, share, part), f32),
             pltpu.VMEM((n_rep, 8, share), f32),
-            pltpu.VMEM((nx, share, width), f32),
-            pltpu.VMEM((nx - 1, share, width), f32),
-            pltpu.VMEM((nx - 1, share, width), f32),
+            pltpu.VMEM((2, nx, share, part), f32),
+            pltpu.VMEM((2, nx - 1, share, part), f32),
+            pltpu.VMEM((2, nx - 1, share, part), f32),
             pltpu.VMEM((n_rep, 8, share), f32),
             pltpu.VMEM((n_rep, 8, share), f32),
             pltpu.VMEM((nx - 1, n_rep, 8, share), f32),
-            dma((n_node,)), dma((n_node,)), dma((n_node,)), dma((n_node,)),
+            dma((2, n_node)), dma((2, n_node)), dma((n_node,)), dma((n_node,)),
             dma((BANDS - 1,)), dma((BANDS - 1,)),
-            dma((nx,)), dma((nx,)),
-            dma((nx - 1,)), dma((nx - 1,)),
+            dma((2, nx)), dma((2, nx)),
+            dma((2, nx - 1)), dma((2, nx - 1)),
             dma, dma,
             dma((nx - 1,)), dma((nx - 1,)),
         ],
         compiler_params=pltpu.CompilerParams(
             collective_id=0, has_side_effects=True, vmem_limit_bytes=40 * 1024 * 1024
         ),
-    )(msg, rows, hot)
+    )(msg0, msg1, rows, hot)
 
 
 ORDER_A = ("core", "x", "lo", "hi")
@@ -184,10 +195,13 @@
     return {"core": 2, "x": n_rep // 2, "lo": n_node // 4, "hi": 4}
 
 
-def finish_kernel(n_node, n_rep, n_sems, ga_ref, gb_ref, cold_ref, hot_ref, oa, ob, ocold, ohot, *scratch):
+def finish_kernel(n_node, n_rep, ga_ref, gb_ref, cold_ref, hot_ref, place_ref, oa, ob, ocold, new_hot, *scratch):
     sizes = sizes_of(n_node, n_rep)
     recv_a, acc_a, recv_b, acc_b = scratch[0:4], scratch[4:8], scratch[8:12], scratch[12:16]
     send_sem, recv_sem = scratch[16:18]
+    band, width = hot_ref.shape
+    tidy = band % 8 == 0
+    ohot, pieces = scratch[18:20] if tidy else (new_hot, None)
     node = lax.axis_index("node")
     rep = lax.axis_index("rep")
     nlo = sizes["lo"]
@@ -260,6 +274,9 @@
         if phase == 2:
             arrive(hot_copies)
             hot_copies = gather_start(ohot, ORDER_A, 1)
+        if phase == 3:
+            arrive(hot_copies)
+            hot_copies = gather_start(ohot, ORDER_A, 0)
     oa[tuple(mine[a] for a in ORDER_A)] = cur_a[...]
     ob[tuple(mine[a] for a in ORDER_B)] = cur_b[...]
     for phase in (3, 2, 1, 0):
@@ -267,16 +284,37 @@
         copies_b = gather_start(ob, ORDER_B, phase)
         if phase == 2:
             arrive(hot_copies)
-            hot_copies = gather_start(ohot, ORDER_A, 0)
+            if tidy:
+                hot_rows = new_hot.shape[0]
+                rows = ohot[...].reshape(hot_rows, width)
+                top = rows.astype(jnp.bfloat16)
+                rest = rows - top.astype(jnp.float32)
+                middle = rest.astype(jnp.bfloat16)
+                low = (rest - middle.astype(jnp.float32)).astype(jnp.bfloat16)
+                pieces[:, :width] = top
+                pieces[:, width : 2 * width] = middle
+                pieces[:, 2 * width :] = low
+                step = hot_rows // 4
+                for part in range(4):
+                    chosen = lax.broadcasted_iota(jnp.int32, (hot_rows, step), 0)
+                    chosen = chosen == place_ref[0:1, part * step : (part + 1) * step]
+                    got = lax.dot_general(
+                        jnp.where(chosen, 1.0, 0.0).astype(jnp.bfloat16),
+                        pieces[...],
+                        (((0,), (0,)), ((), ())),
+                        preferred_element_type=jnp.float32,
+                    )
+                    new_hot[part * step : (part + 1) * step] = (
+                        got[:, :width] + got[:, width : 2 * width] + got[:, 2 * width :]
+                    )
         arrive(copies_a)
         arrive(copies_b)
-    arrive(hot_copies)
     arrive(cold_copies)
     for copy in everything:
         copy.wait_send()
 
 
-def finish(n_node, n_rep, ga, gb, cold, hot):
+def finish(n_node, n_rep, ga, gb, cold, hot, place):
     sizes = sizes_of(n_node, n_rep)
     f32 = jnp.float32
     steps = sum(s - 1 for s in sizes.values())
@@ -290,21 +328,28 @@
             acc.append(pltpu.VMEM(rest, f32))
         scratch += recv + acc
     scratch += [pltpu.SemaphoreType.DMA((n_sems,)), pltpu.SemaphoreType.DMA((n_sems,))]
+    blocks = (*(sizes[a] for a in ORDER_A), *hot.shape)
+    band, width = hot.shape
+    hot_rows = place.shape[1]
+    out_hot = jax.ShapeDtypeStruct(blocks, f32)
+    if band % 8 == 0:
+        out_hot = jax.ShapeDtypeStruct((hot_rows, width), f32)
+        scratch += [pltpu.VMEM(blocks, f32), pltpu.VMEM((hot_rows, 3 * width), jnp.bfloat16)]
     return pl.pallas_call(
-        functools.partial(finish_kernel, n_node, n_rep, n_sems),
+        functools.partial(finish_kernel, n_node, n_rep),
         out_shape=(
             jax.ShapeDtypeStruct(ga.shape, f32),
             jax.ShapeDtypeStruct(gb.shape, f32),
             jax.ShapeDtypeStruct((sizes["x"], 2, *cold.shape), f32),
-            jax.ShapeDtypeStruct((*(sizes[a] for a in ORDER_A), *hot.shape), f32),
+            out_hot,
         ),
-        in_specs=[VMEM] * 4,
+        in_specs=[VMEM] * 5,
         out_specs=(VMEM,) * 4,
         scratch_shapes=scratch,
         compiler_params=pltpu.CompilerParams(
             collective_id=1, has_side_effects=True, vmem_limit_bytes=40 * 1024 * 1024
         ),
-    )(ga, gb, cold, hot)
+    )(ga, gb, cold, hot, place)
 
 
 def on_device(
@@ -350,15 +395,8 @@
     local_row = lax.rem(dst_ids, rows_dev)
     lane = jnp.arange(128, dtype=jnp.int32)[None, :]
     extra = jnp.where(
-        lane == 0,
-        1,
-        jnp.where(
-            lane == 1,
-            lax.div(local_row, 32)[:, None],
-            jnp.where(lane == 2, lax.rem(local_row, 32)[:, None], 0),
-        ),
+        lane == 0, lax.div(local_row, 32)[:, None], jnp.where(lane == 1, lax.rem(local_row, 32)[:, None], 0)
     ).astype(bf16)
-    wide = jnp.concatenate([messages, extra], axis=1)
     hot_place = jnp.where(
         dst_ids >= hot_base, lax.rem(dst_ids - hot_base + hot_rows - me * band, hot_rows), -1
     )
@@ -366,18 +404,28 @@
     event = jnp.arange(events, dtype=jnp.int32)[None, :]
     listed = (flat_list[:, None] == event).astype(bf16)
     hot_match = (jnp.arange(BANDS * band, dtype=jnp.int32)[:, None] == hot_place[None, :]).astype(bf16)
-    sent = jnp.dot(listed, wide, preferred_element_type=f32)
-    hot_part = jnp.dot(hot_match, wide, preferred_element_type=f32)
-    send_msg = sent[:, :msg_width].astype(bf16).reshape(n_node, slot_cap, msg_width)
+    part = msg_width // 2
+    msg0, msg1 = (
+        jnp.dot(listed, messages[:, h * part : (h + 1) * part], preferred_element_type=f32)
+        .astype(bf16)
+        .reshape(n_node, slot_cap, part)
+        for h in range(2)
+    )
+    sent = jnp.dot(listed, extra, preferred_element_type=f32)
+    hot_part = jnp.dot(hot_match, messages, preferred_element_type=f32)
+    hot_number = jnp.sum(hot_match.astype(f32), axis=1)
+    hot_part = jnp.concatenate(
+        [hot_part, jnp.broadcast_to(hot_number[:, None], (BANDS * band, 128))], axis=1
+    )
     slots = jnp.arange(slot_cap, dtype=jnp.int32)
     valid = slots[None, :] < cold_count[:, None]
-    row_at = (sent[:, msg_width + 1] * 32.0 + sent[:, msg_width + 2]).astype(jnp.int32)
+    row_at = (sent[:, 0] * 32.0 + sent[:, 1]).astype(jnp.int32)
     send_row = jnp.where(valid, row_at.reshape(n_node, slot_cap), -1)
     send_row = jnp.pad(send_row, ((0, 0), (0, 128 - slot_cap)), constant_values=-1)
     send_row = jnp.broadcast_to(send_row[:, None, :], (n_node, 8, 128))
 
     cold_total, cold_cnt, hot_sum = exchange(
-        n_node, n_rep, rows_dev, send_msg, send_row, hot_part.reshape(BANDS, band, msg_width + 128)
+        n_node, n_rep, rows_dev, msg0, msg1, send_row, hot_part.reshape(BANDS, band, msg_width + 128)
     )
     first = rep * share
     cold_number = lax.dynamic_index_in_dim(cold_cnt, rep, 0, keepdims=False)[0]
@@ -418,17 +466,19 @@
     piece = g_rows // n_dev
     ga = grads[:, :half].reshape(*(sizes[a] for a in ORDER_A), piece, half)
     gb = grads[:, half:].reshape(*(sizes[a] for a in ORDER_B), piece, half)
-    oa, ob, new_cold, hot_blocks = finish(n_node, n_rep, ga, gb, fresh[:share], fresh[share:])
-    grads = jnp.concatenate([oa.reshape(g_rows, half), ob.reshape(g_rows, half)], axis=1)
-    agg_rows = w_in.shape[0]
-
     ids = hot_ids - hot_base
     block, inner = lax.div(ids, band), lax.rem(ids, band)
     at_node, at_rep = lax.div(block, n_rep), lax.rem(block, n_rep)
     hi, lo = lax.div(at_node, sizes["lo"]), lax.rem(at_node, sizes["lo"])
     xi, core = lax.div(at_rep, 2), lax.rem(at_rep, 2)
     place = (((core * sizes["x"] + xi) * sizes["lo"] + lo) * sizes["hi"] + hi) * band + inner
-    new_hot = jnp.take(hot_blocks.reshape(hot_rows, width), place, axis=0)
+    place_rows = jnp.broadcast_to(place[None, :], (8, hot_rows))
+    oa, ob, new_cold, new_hot = finish(n_node, n_rep, ga, gb, fresh[:share], fresh[share:], place_rows)
+    grads = jnp.concatenate([oa.reshape(g_rows, half), ob.reshape(g_rows, half)], axis=1)
+    agg_rows = w_in.shape[0]
+
+    if band % 8:
+        new_hot = jnp.take(new_hot.reshape(hot_rows, width), place, axis=0)
     return (new_cold.reshape(rows_dev, width), new_hot, grads[:agg_rows], grads[agg_rows:])
 
 

time: 134 us -> 116 us (0.87)
  local copies, waits for them, and re-layouts: 13.1 us -> 3.91 us
  Pallas kernels: 98.1 us -> 91.3 us
  other arithmetic: 9.41 us -> 7.32 us
    pallas_call x1, Pallas kernels: 57.5 us -> 48.7 us  [finish(): pl.pallas_call(functools.partial(finish_kernel, n_node, n_rep), out_shape...]
    gather x1 -> x0, local copies, waits for them, and re-layouts: 4.68 us -> none  [on_device(): new_hot = jnp.take(hot_blocks.reshape(hot_rows, width), place, axis=0)]
    slice x2 -> x0, local copies, waits for them, and re-layouts: 2.8 us -> none  [on_device(): sent[:, :msg_width].astype(bf16).reshape(n_node, slot_cap, msg_width)]
    select_n x1 -> x0, other arithmetic: 2.4 us -> none  [on_device(): new_hot = jnp.take(hot_blocks.reshape(hot_rows, width), place, axis=0)]
    pallas_call x1, Pallas kernels: 40.6 us -> 42.6 us  [exchange(): pl.pallas_call(functools.partial(exchange_kernel, n_node, n_rep), out_sha...]
    unnamed x33 -> x25, local copies, waits for them, and re-layouts: 3.66 us -> 2.68 us
    dot_general x2 -> x4, matrix products: 2.26 us -> 3.12 us  [the longest x2 1.67 us: on_device(): jnp.dot(listed, messages[:, h * part:(h + 1) * part], preferred_element_t...]
where the time goes in v2:
time: 116 us; the launch traced here: 114 us
  Pallas kernels  91.3 us (79%)
  matrix products  10.8 us (9%)
  other arithmetic  7.32 us (6%)
  local copies, waits for them, and re-layouts  3.91 us (3%)
    pallas_call x1, Pallas kernels, finish(): pl.pallas_call(functools.partial(finish_kernel, n_node, n_rep), out_shape...  48.7 us
    pallas_call x1, Pallas kernels, exchange(): pl.pallas_call(functools.partial(exchange_kernel, n_node, n_rep), out_sha...  42.6 us
    unnamed x25, local copies, waits for them, and re-layouts  2.68 us
    dot_general x1, matrix products, on_device(): jnp.dot(own, jnp.concatenate([hot_memory, cot_hot], axis=1), precision=la...  2.44 us

profile of v2, /device:TPU:1, one launch (start us, length us, event | category | flops | bytes accessed | tf_op | source)
XLA Modules:
  0.0 114.4 jit_solution(1259003913172546538)
XLA Ops:
  0.6 0.0 copy-start
  0.6 0.0 copy-start.4
  0.7 0.0 copy-start.5
  0.7 0.0 copy-start.2
  0.7 0.8 convert_element_type.54
  1.5 0.7 fusion.63
  2.2 0.7 fusion.55
  2.9 0.1 convert_reduce_fusion
  3.0 0.0 copy-start.9
  3.0 0.1 broadcast_in_dim.106
  3.1 2.4 %fusion.4 = f32[32,512]{1,0:T(8,128)S(1)} fusion(f32[1024,256]{1,0:T(8,128)} %param.20, f32[1024,256]{1,0:T(8,128)} %param.18, s32[1024]{0:T(1024)} %param.27, s32[32]{0:T(128)S(1)} %iota_add_fusion), kind=kOutput, calls=%fused_computation.10 | convolution fusion | flops 201883648 | bytes 2166912 | tf_op jit(solution)/shard_map/dot_general | solution.py:437
  5.6 0.0 copy-done.4
  5.6 0.0 copy-done.5
  5.6 0.0 copy-start.6
  5.6 0.0 copy-start.3
  5.6 1.9 %cosine_convert_fusion = bf16[1024,128]{0,1:T(8,128)(2,1)S(1)} fusion(f32[128]{0:T(128)S(1)} %copy-done.4, f32[128]{0:T(128)S(1)} %copy-done.5, f32[1024]{0:T(1024)S(1)} %convert_element_type.54), kind=kLoop, calls=%fused_computation.47 | loop fusion | flops 393216 | bytes 267264 | tf_op jit(solution)/shard_map/convert_element_type | solution.py:391
  7.6 0.0 copy-done.2
  7.6 0.1 copy.21
  7.7 0.0 copy-done.9
  7.7 0.0 copy-start.8
  7.8 1.1 fusion
  8.9 0.0 copy-done.6
  8.9 0.1 fusion.67
  9.0 0.0 copy-done.3
  9.0 1.0 constant_dynamic-slice_fusion
  10.0 0.0 copy-done.8
  10.0 0.0 copy-start.7
  10.0 0.0 copy-start.10
  10.1 1.1 fusion.13
  11.2 0.0 copy-done.7
  11.2 0.0 copy-done.10
  11.2 1.0 multiply_convert_fusion
  12.2 0.3 fusion.30
  12.6 0.8 fusion.15
  13.4 0.8 fusion.14
  14.3 42.6 %shard_map.192 = (f32[256,512]{1,0:T(8,128)S(1)}, f32[4,8,256]{2,1,0:T(8,128)S(1)}, f32[32,640]{1,0:T(8,128)S(1)}) custom-call(bf16[8,128,256]{2,1,0:T(8,128)(2,1)S(1)} %bitcast.26, bf16[8,128,256]{2,1,0:T(8,128)(2,1)S(1)} %bitcast.25, s32[8,8,128]{2,1,0:T(8,128)S(1)} %broadcast_in_dim.104.rows_ref, f32[4,32,640]{2,1,0:T(8,128)S(1)} %bitcast.23), custom_call_target="tpu_custom_call" | custom-call | tf_op jit(solution)/shard_map/pallas_call | solution.py:155
  56.9 0.1 slice_reduce_fusion
  57.1 0.0 copy-done
  57.1 0.0 copy-start.1
  57.1 0.4 fusion.78
  57.5 0.5 copy-done.1
  58.1 0.3 fusion.83
  58.3 0.2 add_select_fusion
  58.6 0.2 fusion.80
  58.8 0.1 subtract_multiply_fusion
  59.0 0.9 fusion.24
  59.9 1.5 %fusion.22 = f32[512,768]{1,0:T(8,128)S(1)} fusion(f32[288,256]{1,0:T(8,128)S(1)} %get-tuple-element.21, f32[288,256]{1,0:T(8,128)S(1)} %get-tuple-element.22, f32[288,256]{1,0:T(8,128)S(1)} %subtract_multiply_fusion, f32[32,512]{1,0:T(8,128)S(1)} %slice.68, f32[256,512]{1,0:T(8,128)S(1)} %get-tuple-element.11, f32[288]{0:T(512)S(1)} %fusion.69), kind=kOutput, calls=%fused_computation.31 | convolution fusion | flops 1360060416 | bytes 3048576 | tf_op jit(solution)/shard_map/dot_general | solution.py:460
  61.4 0.2 pad_maximum_fusion
  61.6 48.7 %shard_map.193 = (f32[2,2,2,4,24,384]{5,4,3,2,1,0:T(8,128)S(1)}, f32[2,2,2,4,24,384]{5,4,3,2,1,0:T(8,128)S(1)}, f32[2,2,256,256]{3,2,1,0:T(8,128)S(1)}, f32[1024,256]{1,0:T(8,128)S(1)}) custom-call(f32[2,2,2,4,24,384]{5,4,3,2,1,0:T(8,128)S(1)} %bitcast.22, f32[2,2,2,4,24,384]{5,4,3,2,1,0:T(8,128)S(1)} %bitcast.21, f32[256,256]{1,0:T(8,128)S(1)} %slice.99.cold_ref, ...), custom_call_target="tpu_custom_call" | custom-call | tf_op jit(solution)/shard_map/pallas_call | solution.py:338
  110.3 0.9 pad_maximum_fusion.4
  111.2 1.3 %fusion.12 = f32[512,768]{1,0:T(8,128)} fusion(f32[768,384]{1,0:T(8,128)S(1)} %bitcast.18, f32[768,384]{1,0:T(8,128)S(1)} %bitcast.20), kind=kLoop, calls=%fused_computation.19 | loop fusion | flops 393216 | bytes 3932160 | tf_op jit(solution)/shard_map/concatenate | solution.py:477
  112.5 1.0 copy.24
  113.4 1.0 copy.25
  (14 shorter events, 0.1 us)
Async XLA Ops:
  0.6 56.4 %copy-start = (bf16[512,768]{1,0:T(8,128)(2,1)S(1)}, bf16[512,768]{1,0:T(8,128)(2,1)}, u32[]{:S(2)}) copy-start(bf16[512,768]{1,0:T(8,128)(2,1)} %param.32) | copy-start | bytes 2359300
  0.6 4.9 %copy-start.4 = (f32[128]{0:T(128)S(1)}, f32[128]{0:T(128)}, u32[]{:S(2)}) copy-start(f32[128]{0:T(128)} %param.29) | copy-start | bytes 1540
  0.7 4.9 %copy-start.5 = (f32[128]{0:T(128)S(1)}, f32[128]{0:T(128)}, u32[]{:S(2)}) copy-start(f32[128]{0:T(128)} %param.28) | copy-start | bytes 1540
  0.7 6.9 %copy-start.2 = (bf16[1024,128]{1,0:T(8,128)(2,1)S(1)}, bf16[1024,128]{1,0:T(8,128)(2,1)}, u32[]{:S(2)}) copy-start(bf16[1024,128]{1,0:T(8,128)(2,1)} %param.24) | copy-start | bytes 786436
  3.0 4.7 %copy-start.9 = (s32[8,128]{1,0:T(8,128)S(1)}, s32[8,128]{1,0:T(8,128)}, u32[]{:S(2)}) copy-start(s32[8,128]{1,0:T(8,128)} %param.25) | copy-start | bytes 12292
  5.6 3.3 %copy-start.6 = (s32[8]{0:T(128)S(1)}, s32[8]{0:T(128)}, u32[]{:S(2)}) copy-start(s32[8]{0:T(128)} %param.26) | copy-start | bytes 100
  5.6 3.4 %copy-start.3 = (f32[1024,256]{1,0:T(8,128)S(1)}, f32[1024,256]{1,0:T(8,128)}, u32[]{:S(2)}) copy-start(f32[1024,256]{1,0:T(8,128)} %param.17) | copy-start | bytes 3145732
  7.7 2.3 %copy-start.8 = (s32[1024]{0:T(1024)S(1)}, s32[1024]{0:T(1024)}, u32[]{:S(2)}) copy-start(s32[1024]{0:T(1024)} %param.21) | copy-start | bytes 12292
  10.0 1.1 %copy-start.7 = (bf16[512,512]{1,0:T(8,128)(2,1)S(1)}, bf16[512,512]{1,0:T(8,128)(2,1)}, u32[]{:S(2)}) copy-start(bf16[512,512]{1,0:T(8,128)(2,1)} %param.30) | copy-start | bytes 1572868
  10.0 1.1 %copy-start.10 = (f32[512]{0:T(512)S(1)}, f32[512]{0:T(512)}, u32[]{:S(2)}) copy-start(f32[512]{0:T(512)} %param.31) | copy-start | bytes 6148
  57.1 1.0 copy-start.1

commit v3 on v2

--- a/solution.py
+++ b/solution.py
@@ -1,4 +1,5 @@
 import functools
+import math
 
 import jax
 import jax.numpy as jnp
@@ -189,19 +190,30 @@
 
 ORDER_A = ("core", "x", "lo", "hi")
 ORDER_B = ("core", "lo", "x", "hi")
+ORDER_HOT = ("core", "lo", "hi", "x")
+LANES = 128
 
 
 def sizes_of(n_node, n_rep):
     return {"core": 2, "x": n_rep // 2, "lo": n_node // 4, "hi": 4}
 
 
-def finish_kernel(n_node, n_rep, ga_ref, gb_ref, cold_ref, hot_ref, place_ref, oa, ob, ocold, new_hot, *scratch):
+def span(sizes, order, phase):
+    return math.prod(sizes[a] for a in order[phase + 1 :])
+
+
+def parts_of(columns):
+    return [(first, ORDER_B if i % 2 else ORDER_A) for i, first in enumerate(range(0, columns, LANES))]
+
+
+def finish_kernel(n_node, n_rep, g_ref, cold_ref, hot_ref, place_ref, og, ocold, new_hot, *scratch):
     sizes = sizes_of(n_node, n_rep)
-    recv_a, acc_a, recv_b, acc_b = scratch[0:4], scratch[4:8], scratch[8:12], scratch[12:16]
-    send_sem, recv_sem = scratch[16:18]
+    parts = parts_of(g_ref.shape[2])
+    send_sem, recv_sem = scratch[:2]
+    buffers = scratch[2 : 2 + 8 * len(parts)]
     band, width = hot_ref.shape
     tidy = band % 8 == 0
-    ohot, pieces = scratch[18:20] if tidy else (new_hot, None)
+    ohot, pieces = scratch[2 + 8 * len(parts) :] if tidy else (new_hot, None)
     node = lax.axis_index("node")
     rep = lax.axis_index("rep")
     nlo = sizes["lo"]
@@ -214,123 +226,130 @@
 
     greet([peer(axis, k) for axis in ORDER_A for k in range(1, sizes[axis])])
 
-    used = [0]
     everything = []
 
     def ship(src, dst, device):
-        i = used[0]
-        used[0] += 1
+        i = len(everything)
         copy = push(src, dst, send_sem.at[i], recv_sem.at[i], device)
         everything.append(copy)
         return copy
 
-    def scatter_start(cur, recv, axis):
-        size = sizes[axis]
+    def arrive(copies):
+        for copy in copies:
+            copy.wait_recv()
+
+    def held(part, phase):
+        first, order = parts[part]
+        if phase == 0:
+            return lambda i, n: g_ref.at[pl.ds(i, n), :, pl.ds(first, LANES)]
+        acc = buffers[8 * part + 2 * (phase - 1) + 1]
+        return lambda i, n: acc.at[pl.ds(i, n)]
+
+    def scatter_start(part, phase):
+        order = parts[part][1]
+        axis = order[phase]
+        size, n = sizes[axis], span(sizes, order, phase)
+        view, recv = held(part, phase), buffers[8 * part + 2 * phase]
         return [
-            ship(cur.at[lax.rem(mine[axis] + k, size)], recv.at[k - 1], peer(axis, k)) for k in range(1, size)
+            ship(view(lax.rem(mine[axis] + k, size) * n, n), recv.at[k - 1], peer(axis, k)) for k in range(1, size)
         ]
 
-    def scatter_end(copies, cur, recv, acc, axis):
-        total = cur[mine[axis]]
+    def scatter_end(part, phase, copies):
+        order = parts[part][1]
+        axis = order[phase]
+        n = span(sizes, order, phase)
+        recv, acc = buffers[8 * part + 2 * phase], buffers[8 * part + 2 * phase + 1]
+        total = held(part, phase)(mine[axis] * n, n)[...]
         for k, copy in enumerate(copies):
             copy.wait_recv()
             total = total + recv[k]
         acc[...] = total
 
-    def gather_start(out, order, phase):
+    def prefix(order, phase):
+        return sum(mine[order[i]] * span(sizes, order, i) for i in range(phase + 1))
+
+    def gather_start(part, phase):
+        first, order = parts[part]
         axis = order[phase]
-        where = out.at[tuple(mine[a] for a in order[: phase + 1])]
+        where = og.at[pl.ds(prefix(order, phase), span(sizes, order, phase)), :, pl.ds(first, LANES)]
         return [ship(where, where, peer(axis, k)) for k in range(1, sizes[axis])]
 
-    def arrive(copies):
-        for copy in copies:
-            copy.wait_recv()
-
+    def hot_start(phase):
+        axis = ORDER_HOT[phase]
+        where = ohot.at[pl.ds(prefix(ORDER_HOT, phase), span(sizes, ORDER_HOT, phase))]
+        return [ship(where, where, peer(axis, k)) for k in range(1, sizes[axis])]
+
+    everyone = range(len(parts))
+    flying = [scatter_start(part, 0) for part in everyone]
     ocold[mine["x"], mine["core"]] = cold_ref[...]
-    ohot[tuple(mine[a] for a in ORDER_A)] = hot_ref[...]
+    ohot[prefix(ORDER_HOT, 3)] = hot_ref[...]
     cold_place = ocold.at[mine["x"], mine["core"]]
-    first_a = scatter_start(ga_ref, recv_a[0], ORDER_A[0])
-    first_b = scatter_start(gb_ref, recv_b[0], ORDER_B[0])
+    hot_copies = hot_start(3)
     cold_copies = [ship(cold_place, cold_place, peer("x", k)) for k in range(1, sizes["x"])]
-    hot_copies = gather_start(ohot, ORDER_A, 3)
-
-    cur_a, cur_b, copies_a, copies_b = ga_ref, gb_ref, first_a, first_b
+
     for phase in range(4):
-        scatter_end(copies_a, cur_a, recv_a[phase], acc_a[phase], ORDER_A[phase])
-        cur_a = acc_a[phase]
-        if phase < 3:
-            copies_a = scatter_start(cur_a, recv_a[phase + 1], ORDER_A[phase + 1])
-        scatter_end(copies_b, cur_b, recv_b[phase], acc_b[phase], ORDER_B[phase])
-        cur_b = acc_b[phase]
-        if phase < 3:
-            copies_b = scatter_start(cur_b, recv_b[phase + 1], ORDER_B[phase + 1])
-        if phase == 0:
-            arrive(hot_copies)
-            hot_copies = gather_start(ohot, ORDER_A, 2)
+        for part in everyone:
+            scatter_end(part, phase, flying[part])
+            if phase < 3:
+                flying[part] = scatter_start(part, phase + 1)
+            else:
+                first, order = parts[part]
+                og[pl.ds(prefix(order, 3), 1), :, first : first + LANES] = buffers[8 * part + 7][...]
+                flying[part] = gather_start(part, 3)
+        arrive(hot_copies)
+        hot_copies = hot_start(2 - phase) if phase < 3 else []
         if phase == 1:
             arrive(cold_copies)
             side = ocold.at[:, mine["core"]]
             cold_copies = [ship(side, side, peer("core", 1))]
-        if phase == 2:
-            arrive(hot_copies)
-            hot_copies = gather_start(ohot, ORDER_A, 1)
-        if phase == 3:
-            arrive(hot_copies)
-            hot_copies = gather_start(ohot, ORDER_A, 0)
-    oa[tuple(mine[a] for a in ORDER_A)] = cur_a[...]
-    ob[tuple(mine[a] for a in ORDER_B)] = cur_b[...]
+    if tidy:
+        hot_rows = new_hot.shape[0]
+        rows = ohot[...].reshape(hot_rows, width)
+        top = rows.astype(jnp.bfloat16)
+        rest = rows - top.astype(jnp.float32)
+        middle = rest.astype(jnp.bfloat16)
+        pieces[:, :width] = top
+        pieces[:, width : 2 * width] = middle
+        pieces[:, 2 * width :] = (rest - middle.astype(jnp.float32)).astype(jnp.bfloat16)
+
+    def permute_hot(part):
+        step = new_hot.shape[0] // 4
+        chosen = lax.broadcasted_iota(jnp.int32, (new_hot.shape[0], step), 0)
+        chosen = chosen == place_ref[0:1, part * step : (part + 1) * step]
+        got = lax.dot_general(
+            jnp.where(chosen, 1.0, 0.0).astype(jnp.bfloat16),
+            pieces[...],
+            (((0,), (0,)), ((), ())),
+            preferred_element_type=jnp.float32,
+        )
+        new_hot[part * step : (part + 1) * step] = got[:, :width] + got[:, width : 2 * width] + got[:, 2 * width :]
+
     for phase in (3, 2, 1, 0):
-        copies_a = gather_start(oa, ORDER_A, phase)
-        copies_b = gather_start(ob, ORDER_B, phase)
-        if phase == 2:
-            arrive(hot_copies)
-            if tidy:
-                hot_rows = new_hot.shape[0]
-                rows = ohot[...].reshape(hot_rows, width)
-                top = rows.astype(jnp.bfloat16)
-                rest = rows - top.astype(jnp.float32)
-                middle = rest.astype(jnp.bfloat16)
-                low = (rest - middle.astype(jnp.float32)).astype(jnp.bfloat16)
-                pieces[:, :width] = top
-                pieces[:, width : 2 * width] = middle
-                pieces[:, 2 * width :] = low
-                step = hot_rows // 4
-                for part in range(4):
-                    chosen = lax.broadcasted_iota(jnp.int32, (hot_rows, step), 0)
-                    chosen = chosen == place_ref[0:1, part * step : (part + 1) * step]
-                    got = lax.dot_general(
-                        jnp.where(chosen, 1.0, 0.0).astype(jnp.bfloat16),
-                        pieces[...],
-                        (((0,), (0,)), ((), ())),
-                        preferred_element_type=jnp.float32,
-                    )
-                    new_hot[part * step : (part + 1) * step] = (
-                        got[:, :width] + got[:, width : 2 * width] + got[:, 2 * width :]
-                    )
-        arrive(copies_a)
-        arrive(copies_b)
+        for part in everyone:
+            arrive(flying[part])
+            flying[part] = gather_start(part, phase - 1) if phase else []
+        if tidy:
+            permute_hot(3 - phase)
     arrive(cold_copies)
     for copy in everything:
         copy.wait_send()
 
 
-def finish(n_node, n_rep, ga, gb, cold, hot, place):
+def finish(n_node, n_rep, grads, cold, hot, place):
     sizes = sizes_of(n_node, n_rep)
     f32 = jnp.float32
+    n_dev, piece, columns = grads.shape
+    parts = parts_of(columns)
     steps = sum(s - 1 for s in sizes.values())
-    n_sems = 4 * steps + sizes["x"] - 1 + 1 + steps
-    scratch = []
-    for part, order in ((ga, ORDER_A), (gb, ORDER_B)):
-        recv, acc = [], []
+    n_sems = 2 * steps * len(parts) + steps + sizes["x"] - 1 + 1
+    scratch = [pltpu.SemaphoreType.DMA((n_sems,)), pltpu.SemaphoreType.DMA((n_sems,))]
+    for first, order in parts:
         for phase in range(4):
-            rest = part.shape[phase + 1 :]
-            recv.append(pltpu.VMEM((sizes[order[phase]] - 1, *rest), f32))
-            acc.append(pltpu.VMEM(rest, f32))
-        scratch += recv + acc
-    scratch += [pltpu.SemaphoreType.DMA((n_sems,)), pltpu.SemaphoreType.DMA((n_sems,))]
-    blocks = (*(sizes[a] for a in ORDER_A), *hot.shape)
+            block = (span(sizes, order, phase), piece, LANES)
+            scratch += [pltpu.VMEM((sizes[order[phase]] - 1, *block), f32), pltpu.VMEM(block, f32)]
     band, width = hot.shape
     hot_rows = place.shape[1]
+    blocks = (n_dev, band, width)
     out_hot = jax.ShapeDtypeStruct(blocks, f32)
     if band % 8 == 0:
         out_hot = jax.ShapeDtypeStruct((hot_rows, width), f32)
@@ -338,18 +357,17 @@
     return pl.pallas_call(
         functools.partial(finish_kernel, n_node, n_rep),
         out_shape=(
-            jax.ShapeDtypeStruct(ga.shape, f32),
-            jax.ShapeDtypeStruct(gb.shape, f32),
+            jax.ShapeDtypeStruct(grads.shape, f32),
             jax.ShapeDtypeStruct((sizes["x"], 2, *cold.shape), f32),
             out_hot,
         ),
-        in_specs=[VMEM] * 5,
-        out_specs=(VMEM,) * 4,
+        in_specs=[VMEM] * 4,
+        out_specs=(VMEM,) * 3,
         scratch_shapes=scratch,
         compiler_params=pltpu.CompilerParams(
             collective_id=1, has_side_effects=True, vmem_limit_bytes=40 * 1024 * 1024
         ),
-    )(ga, gb, cold, hot, place)
+    )(grads, cold, hot, place)
 
 
 def on_device(
@@ -460,23 +478,24 @@
     grad_a = jnp.dot(agg.astype(f32).T, d_input, precision=lax.Precision.HIGHEST)
     grad_b = jnp.dot(mem_wide.T, d_hidden, precision=lax.Precision.HIGHEST)
     grads = jnp.concatenate([grad_a, grad_b], axis=0)
-    g_rows, g_cols = grads.shape
-    half = g_cols // 2
     sizes = sizes_of(n_node, n_rep)
-    piece = g_rows // n_dev
-    ga = grads[:, :half].reshape(*(sizes[a] for a in ORDER_A), piece, half)
-    gb = grads[:, half:].reshape(*(sizes[a] for a in ORDER_B), piece, half)
     ids = hot_ids - hot_base
     block, inner = lax.div(ids, band), lax.rem(ids, band)
     at_node, at_rep = lax.div(block, n_rep), lax.rem(block, n_rep)
-    hi, lo = lax.div(at_node, sizes["lo"]), lax.rem(at_node, sizes["lo"])
-    xi, core = lax.div(at_rep, 2), lax.rem(at_rep, 2)
-    place = (((core * sizes["x"] + xi) * sizes["lo"] + lo) * sizes["hi"] + hi) * band + inner
+    spot = {
+        "hi": lax.div(at_node, sizes["lo"]),
+        "lo": lax.rem(at_node, sizes["lo"]),
+        "x": lax.div(at_rep, 2),
+        "core": lax.rem(at_rep, 2),
+    }
+    place = sum(spot[a] * span(sizes, ORDER_HOT, i) for i, a in enumerate(ORDER_HOT)) * band + inner
     place_rows = jnp.broadcast_to(place[None, :], (8, hot_rows))
-    oa, ob, new_cold, new_hot = finish(n_node, n_rep, ga, gb, fresh[:share], fresh[share:], place_rows)
-    grads = jnp.concatenate([oa.reshape(g_rows, half), ob.reshape(g_rows, half)], axis=1)
+    g_rows, g_cols = grads.shape
+    grads, new_cold, new_hot = finish(
+        n_node, n_rep, grads.reshape(n_dev, g_rows // n_dev, g_cols), fresh[:share], fresh[share:], place_rows
+    )
+    grads = grads.reshape(g_rows, g_cols)
     agg_rows = w_in.shape[0]
-
     if band % 8:
         new_hot = jnp.take(new_hot.reshape(hot_rows, width), place, axis=0)
     return (new_cold.reshape(rows_dev, width), new_hot, grads[:agg_rows], grads[agg_rows:])

time: 116 us -> 112 us (0.966)
  Pallas kernels: 91.3 us -> 88.6 us
  other arithmetic: 7.32 us -> 5.15 us
  local copies, waits for them, and re-layouts: 3.91 us -> 5.9 us
    pallas_call x1, Pallas kernels: 48.7 us -> 46 us  [finish(): pl.pallas_call(functools.partial(finish_kernel, n_node, n_rep), out_shape...]
    concatenate x2 -> x0, other arithmetic: 2.19 us -> none  [on_device(): jnp.concatenate([oa.reshape(g_rows, half), ob.reshape(g_rows, half)], axi...]
    slice x0 -> x2, local copies, waits for them, and re-layouts: none -> 2.17 us  [the longest x1 1.24 us: on_device(): grads[:agg_rows]]
where the time goes in v3:
time: 112 us
  Pallas kernels  88.6 us (79%)
  matrix products  10.8 us (10%)
  local copies, waits for them, and re-layouts  5.9 us (5%)
  other arithmetic  5.15 us (5%)
    pallas_call x1, Pallas kernels, finish(): pl.pallas_call(functools.partial(finish_kernel, n_node, n_rep), out_shape...  46 us
    pallas_call x1, Pallas kernels, exchange(): pl.pallas_call(functools.partial(exchange_kernel, n_node, n_rep), out_sha...  42.6 us
    unnamed x25, local copies, waits for them, and re-layouts  2.5 us
    dot_general x1, matrix products, on_device(): jnp.dot(own, jnp.concatenate([hot_memory, cot_hot], axis=1), precision=la...  2.44 us

profile of v3, /device:TPU:1, one launch (start us, length us, event | category | flops | bytes accessed | tf_op | source)
XLA Modules:
  0.0 111.5 jit_solution(12561349574526273249)
XLA Ops:
  0.6 0.0 copy-start
  0.6 0.0 copy-start.4
  0.7 0.0 copy-start.5
  0.7 0.0 copy-start.9
  0.7 0.0 copy-start.2
  0.7 0.8 convert_element_type.54
  1.5 0.7 fusion.59
  2.2 0.7 fusion.53
  2.9 0.1 convert_reduce_fusion
  3.0 0.1 broadcast_in_dim.106
  3.1 2.4 %fusion.4 = f32[32,512]{1,0:T(8,128)S(1)} fusion(f32[1024,256]{1,0:T(8,128)} %param.20, f32[1024,256]{1,0:T(8,128)} %param.18, s32[1024]{0:T(1024)} %param.27, s32[32]{0:T(128)S(1)} %iota_add_fusion), kind=kOutput, calls=%fused_computation.7 | convolution fusion | flops 201883648 | bytes 2166912 | tf_op jit(solution)/shard_map/dot_general | solution.py:455
  5.6 0.0 copy-start.6
  5.6 0.0 copy-start.3
  5.6 0.0 copy-done.4
  5.6 0.0 copy-done.5
  5.6 1.9 %cosine_convert_fusion = bf16[1024,128]{0,1:T(8,128)(2,1)S(1)} fusion(f32[128]{0:T(128)S(1)} %copy-done.4, f32[128]{0:T(128)S(1)} %copy-done.5, f32[1024]{0:T(1024)S(1)} %convert_element_type.54), kind=kLoop, calls=%fused_computation.40 | loop fusion | flops 393216 | bytes 267264 | tf_op jit(solution)/shard_map/convert_element_type | solution.py:409
  7.6 0.0 copy-done.2
  7.6 0.1 copy.21
  7.7 0.0 copy-done.9
  7.7 0.0 copy-start.8
  7.8 1.1 %fusion = f32[1024,128]{0,1:T(8,128)S(1)} fusion(s32[1024]{0:T(1024)S(1)} %bitcast.25, s32[1024]{0:T(1024)S(1)} %get-tuple-element.25, s32[1024]{0:T(1024)S(1)} %get-tuple-element.24, pred[128]{0:T(512)(128)(4,1)S(1)} %get-tuple-element.28, pred[128]{0:T(512)(128)(4,1)S(1)} %get-tuple-element.29), kind=kOutput, calls=%fused_computation.2 | convolution fusion | flops 269877248 | bytes 536832 | tf_op jit(solution)/shard_map/dot_general | solution.py:432
  8.9 0.0 copy-done.6
  8.9 0.1 fusion.65
  9.0 0.0 copy-done.3
  9.0 1.0 constant_dynamic-slice_fusion
  10.0 0.0 copy-start.7
  10.0 0.0 copy-start.10
  10.0 0.0 copy-done.8
  10.1 1.1 fusion.12
  11.2 0.0 copy-done.7
  11.2 0.0 copy-done.10
  11.2 1.0 multiply_convert_fusion
  12.3 0.3 fusion.28
  12.6 0.8 fusion.14
  13.4 0.8 fusion.13
  14.3 42.6 %shard_map.192 = (f32[256,512]{1,0:T(8,128)S(1)}, f32[4,8,256]{2,1,0:T(8,128)S(1)}, f32[32,640]{1,0:T(8,128)S(1)}) custom-call(bf16[8,128,256]{2,1,0:T(8,128)(2,1)S(1)} %bitcast.21, bf16[8,128,256]{2,1,0:T(8,128)(2,1)S(1)} %bitcast.20, s32[8,8,128]{2,1,0:T(8,128)S(1)} %broadcast_in_dim.104.rows_ref, f32[4,32,640]{2,1,0:T(8,128)S(1)} %bitcast.18), custom_call_target="tpu_custom_call" | custom-call | tf_op jit(solution)/shard_map/pallas_call | solution.py:156
  56.9 0.0 copy-start.1
  56.9 0.1 slice_reduce_fusion
  57.1 0.0 copy-done
  57.1 0.4 fusion.76
  57.5 0.4 copy-done.1
  57.9 0.3 fusion.81
  58.2 0.2 add_select_fusion
  58.4 0.3 subtract_multiply_fusion
  58.7 0.1 fusion.78
  58.8 0.9 fusion.22
  59.7 1.5 %fusion.20 = f32[512,768]{1,0:T(8,128)S(1)} fusion(f32[288,256]{1,0:T(8,128)S(1)} %get-tuple-element.19, f32[288,256]{1,0:T(8,128)S(1)} %get-tuple-element.20, f32[288,256]{1,0:T(8,128)S(1)} %get-tuple-element.18, f32[32,512]{1,0:T(8,128)S(1)} %slice.62, f32[256,512]{1,0:T(8,128)S(1)} %get-tuple-element.10, f32[288]{0:T(512)S(1)} %fusion.67), kind=kOutput, calls=%fused_computation.25 | convolution fusion | flops 1360060416 | bytes 3048576 | tf_op jit(solution)/shard_map/dot_general | solution.py:478
  61.2 0.2 pad_maximum_fusion
  61.4 46.0 %shard_map.193 = (f32[32,24,768]{2,1,0:T(8,128)S(1)}, f32[2,2,256,256]{3,2,1,0:T(8,128)S(1)}, f32[1024,256]{1,0:T(8,128)S(1)}) custom-call(f32[32,24,768]{2,1,0:T(8,128)S(1)} %bitcast.15, f32[256,256]{1,0:T(8,128)S(1)} %slice.89.cold_ref, f32[32,256]{1,0:T(8,128)S(1)} %slice.90.hot_ref, s32[8,1024]{1,0:T(8,128)S(1)} %broadcast_in_dim.109.place_ref), custom_call_target="tpu_custom_call" | custom-call | tf_op jit(solution)/shard_map/pallas_call | solution.py:357
  107.4 0.9 slice.92
  108.3 1.2 %slice.91 = f32[512,768]{1,0:T(8,128)} slice(f32[768,768]{1,0:T(8,128)S(1)} %bitcast.17), slice={[0:512], [0:768]} | slice | bytes 3145728 | tf_op jit(solution)/shard_map/slice | solution.py:501
  109.6 1.0 copy.24
  110.5 1.0 copy.25
  (14 shorter events, 0.1 us)
Async XLA Ops:
  0.6 56.4 %copy-start = (bf16[512,768]{1,0:T(8,128)(2,1)S(1)}, bf16[512,768]{1,0:T(8,128)(2,1)}, u32[]{:S(2)}) copy-start(bf16[512,768]{1,0:T(8,128)(2,1)} %param.32) | copy-start | bytes 2359300
  0.6 5.0 %copy-start.4 = (f32[128]{0:T(128)S(1)}, f32[128]{0:T(128)}, u32[]{:S(2)}) copy-start(f32[128]{0:T(128)} %param.29) | copy-start | bytes 1540
  0.7 5.0 %copy-start.5 = (f32[128]{0:T(128)S(1)}, f32[128]{0:T(128)}, u32[]{:S(2)}) copy-start(f32[128]{0:T(128)} %param.28) | copy-start | bytes 1540
  0.7 7.1 %copy-start.9 = (s32[8,128]{1,0:T(8,128)S(1)}, s32[8,128]{1,0:T(8,128)}, u32[]{:S(2)}) copy-start(s32[8,128]{1,0:T(8,128)} %param.25) | copy-start | bytes 12292
  0.7 6.9 %copy-start.2 = (bf16[1024,128]{1,0:T(8,128)(2,1)S(1)}, bf16[1024,128]{1,0:T(8,128)(2,1)}, u32[]{:S(2)}) copy-start(bf16[1024,128]{1,0:T(8,128)(2,1)} %param.24) | copy-start | bytes 786436
  5.6 3.4 %copy-start.6 = (s32[8]{0:T(128)S(1)}, s32[8]{0:T(128)}, u32[]{:S(2)}) copy-start(s32[8]{0:T(128)} %param.26) | copy-start | bytes 100
  5.6 3.4 %copy-start.3 = (f32[1024,256]{1,0:T(8,128)S(1)}, f32[1024,256]{1,0:T(8,128)}, u32[]{:S(2)}) copy-start(f32[1024,256]{1,0:T(8,128)} %param.17) | copy-start | bytes 3145732
  7.7 2.3 %copy-start.8 = (s32[1024]{0:T(1024)S(1)}, s32[1024]{0:T(1024)}, u32[]{:S(2)}) copy-start(s32[1024]{0:T(1024)} %param.21) | copy-start | bytes 12292
  10.0 1.2 %copy-start.7 = (bf16[512,512]{1,0:T(8,128)(2,1)S(1)}, bf16[512,512]{1,0:T(8,128)(2,1)}, u32[]{:S(2)}) copy-start(bf16[512,512]{1,0:T(8,128)(2,1)} %param.30) | copy-start | bytes 1572868
  10.0 1.2 %copy-start.10 = (f32[512]{0:T(512)S(1)}, f32[512]{0:T(512)}, u32[]{:S(2)}) copy-start(f32[512]{0:T(512)} %param.31) | copy-start | bytes 6148
  56.9 1.0 copy-start.1

commit v4 on v3

--- a/solution.py
+++ b/solution.py
@@ -31,8 +31,9 @@
 
 def exchange_kernel(
     n_node, n_rep,
-    msg0_ref, msg1_ref, rows_ref, hot_ref,
-    sum_out, cnt_out, hot_out,
+    messages_ref, list_ref, number_ref, dst_ref, ids_ref, memory_any, cot_any, hot_memory_any, hot_cot_any,
+    sum_out, cnt_out, hot_out, mem_out, cot_out,
+    msg0_ref, msg1_ref, rows_ref, hot_ref, hot_state, own_sem,
     recv0, recv1, rows_recv, hot_recv, sums, cnts, core_recv, x_send, x_recv, cnt_core, cnt_send, cnt_x,
     msg_s, msg_r, row_s, row_r, hot_s, hot_r, core_s, core_r, x_s, x_r, cc_s, cc_r, cx_s, cx_r,
 ):
@@ -45,9 +46,33 @@
     me = node * n_rep + rep
     cap, part = msg0_ref.shape[1:]
     share = sum_out.shape[0]
-
-    def at_node(k):
-        return (lax.rem(node + k, n_node), rep)
+    rows_dev = share * n_rep
+    events = messages_ref.shape[0]
+    hot_rows = ids_ref.shape[1]
+    band = hot_rows // n_dev
+    hot_base = n_node * rows_dev
+    f32, bf16 = jnp.float32, jnp.bfloat16
+    nlo = n_node // 4
+    hi, lo = lax.div(node, nlo), lax.rem(node, nlo)
+    steps = [(a, b) for a in (2, 1, 3, 0) for b in range(nlo) if a or b]
+
+    def node_at(a, b):
+        return lax.rem(hi + a, 4) * nlo + lax.rem(lo + b, nlo)
+
+    first = pl.multiple_of(rep * share, share)
+    own_copies = [
+        pltpu.make_async_copy(src, dst, own_sem.at[i])
+        for i, (src, dst) in enumerate(
+            (
+                (memory_any.at[pl.ds(first, share)], mem_out.at[pl.ds(0, share)]),
+                (cot_any.at[pl.ds(first, share)], cot_out.at[pl.ds(0, share)]),
+                (hot_memory_any, hot_state.at[0]),
+                (hot_cot_any, hot_state.at[1]),
+            )
+        )
+    ]
+    for copy in own_copies:
+        copy.start()
 
     def at_linear(k):
         other = lax.rem(me + k, n_dev)
@@ -59,28 +84,68 @@
         return (node, lax.rem(xi + k, nx) * 2 + core)
 
     greet(
-        [at_node(k) for k in range(1, n_node)]
+        [(node_at(a, b), rep) for a, b in steps]
         + [other_core]
         + [at_x(k) for k in range(1, nx)]
         + [at_linear(j) for j in range(1, BANDS)]
         + [at_linear(n_dev - j) for j in range(1, BANDS)]
     )
 
-    sent = []
+    dst = dst_ref[...]
+    local_row = lax.rem(dst, rows_dev)
+    which = lax.broadcasted_iota(jnp.int32, (8, events), 0)
+    high = lax.div(local_row, 32)
+    digits = jnp.where(which == 0, high, jnp.where(which == 1, local_row - high * 32, 0))
+    digits = digits.astype(f32).astype(bf16)
+    slot = lax.broadcasted_iota(jnp.int32, (1, cap), 1)
+
+    def build(other):
+        listed = lax.broadcasted_iota(jnp.int32, (events, cap), 0) == list_ref[pl.ds(other, 1), :]
+        listed = jnp.where(listed, 1.0, 0.0).astype(bf16)
+        block = lax.dot_general(
+            listed, messages_ref[...], (((0,), (0,)), ((), ())), preferred_element_type=f32
+        ).astype(bf16)
+        msg0_ref[other] = block[:, :part]
+        msg1_ref[other] = block[:, part:]
+        found = jnp.dot(digits, listed, preferred_element_type=f32)
+        row = (found[0:1] * 32.0 + found[1:2]).astype(jnp.int32)
+        row = jnp.where(slot < number_ref[pl.ds(other, 1), :], row, -1)
+        rows_ref[other, :, :cap] = jnp.broadcast_to(row, (8, cap))
+
     arrivals = {}
-    for k in range(1, n_node):
-        other = lax.rem(node + k, n_node)
-        arrivals["row", k] = push(rows_ref.at[other], rows_recv.at[node], row_s.at[k], row_r.at[k], at_node(k))
-    for h, (src, dst) in enumerate(((msg0_ref, recv0), (msg1_ref, recv1))):
-        for k in range(1, n_node):
-            other = lax.rem(node + k, n_node)
-            arrivals[h, k] = push(src.at[other], dst.at[node], msg_s.at[h, k], msg_r.at[h, k], at_node(k))
-    sent += list(arrivals.values())
+    for k, (a, b) in enumerate(steps):
+        other = node_at(a, b)
+        build(other)
+        arrivals["row", k] = push(rows_ref.at[other], rows_recv.at[node], row_s.at[k], row_r.at[k], (other, rep))
+        arrivals[0, k] = push(msg0_ref.at[other], recv0.at[node], msg_s.at[0, k], msg_r.at[0, k], (other, rep))
+    for k, (a, b) in enumerate(steps):
+        other = node_at(a, b)
+        arrivals[1, k] = push(msg1_ref.at[other], recv1.at[node], msg_s.at[1, k], msg_r.at[1, k], (other, rep))
+    sent = list(arrivals.values())
+
+    place = dst - hot_base - me * band
+    place = jnp.where(place < 0, place + hot_rows, place)
+    place = jnp.where(dst >= hot_base, place, -1)
+    match = jnp.where(lax.broadcasted_iota(jnp.int32, (BANDS * band, events), 0) == place, 1.0, 0.0)
+    hot_part = jnp.dot(match.astype(bf16), messages_ref[...], preferred_element_type=f32)
+    hot_number = jnp.sum(match, axis=1, keepdims=True)
+    for j in range(BANDS):
+        hot_ref[j, :, : 2 * part] = hot_part[j * band : (j + 1) * band]
+        hot_ref[j, :, 2 * part :] = jnp.broadcast_to(hot_number[j * band : (j + 1) * band], (band, 128))
     hots = [
         push(hot_ref.at[j], hot_recv.at[j - 1], hot_s.at[j - 1], hot_r.at[j - 1], at_linear(j))
         for j in range(1, BANDS)
     ]
     sent += hots
+    build(node)
+    for copy in own_copies:
+        copy.wait()
+    own_rows = max(band, 8)
+    own = lax.broadcasted_iota(jnp.int32, (own_rows, hot_rows), 0) + (hot_base + me * band) == ids_ref[...]
+    own = jnp.where(own, 1.0, 0.0)
+    for i, out in enumerate((mem_out, cot_out)):
+        rows = jnp.dot(own, hot_state[i], precision=lax.Precision.HIGHEST, preferred_element_type=f32)
+        out[share : share + band] = rows[:band]
 
     sums[...] = jnp.zeros_like(sums)
     cnts[...] = jnp.zeros_like(cnts)
@@ -100,11 +165,11 @@
     counts = []
     for h, (mine, got) in enumerate(((msg0_ref, recv0), (msg1_ref, recv1))):
         add_block(h, rows_ref[node, 0:1, :cap], mine[node])
-        for k in range(1, n_node):
+        for k, (a, b) in enumerate(steps):
             if h == 0:
                 arrivals["row", k].wait_recv()
             arrivals[h, k].wait_recv()
-            origin = lax.rem(node + n_node - k, n_node)
+            origin = node_at(4 - a, nlo - b)
             add_block(h, rows_recv[origin, 0:1, :cap], got[origin])
         halves = []
         for k in [*range(1, nx), 0]:
@@ -146,26 +211,40 @@
         copy.wait_send()
 
 
-def exchange(n_node, n_rep, rows_dev, msg0, msg1, rows, hot):
+def exchange(n_node, n_rep, messages, lists, numbers, dst, ids, memory, cot, hot_memory, hot_cot):
     nx = n_rep // 2
-    part = msg0.shape[2]
-    band, hot_width = hot.shape[1:]
+    cap = lists.shape[1]
+    part = messages.shape[1] // 2
+    rows_dev, width = memory.shape
+    hot_rows = hot_memory.shape[0]
+    band = hot_rows // (n_node * n_rep)
+    hot_width = 2 * part + 128
     share = rows_dev // n_rep
     dma = pltpu.SemaphoreType.DMA
     f32 = jnp.float32
+    block = pltpu.VMEM((n_node, cap, part), messages.dtype)
+    row_block = pltpu.VMEM((n_node, 8, 128), jnp.int32)
     return pl.pallas_call(
         functools.partial(exchange_kernel, n_node, n_rep),
         out_shape=(
             jax.ShapeDtypeStruct((share, 2 * part), f32),
             jax.ShapeDtypeStruct((n_rep, 8, share), f32),
             jax.ShapeDtypeStruct((band, hot_width), f32),
+            jax.ShapeDtypeStruct((share + band, width), f32),
+            jax.ShapeDtypeStruct((share + band, width), f32),
         ),
-        in_specs=[VMEM] * 4,
-        out_specs=(VMEM,) * 3,
+        in_specs=[VMEM] * 5 + [pl.BlockSpec(memory_space=pl.ANY)] * 4,
+        out_specs=(VMEM,) * 5,
         scratch_shapes=[
-            pltpu.VMEM(msg0.shape, msg0.dtype),
-            pltpu.VMEM(msg1.shape, msg1.dtype),
-            pltpu.VMEM(rows.shape, rows.dtype),
+            block,
+            block,
+            row_block,
+            pltpu.VMEM((BANDS, band, hot_width), f32),
+            pltpu.VMEM((2, hot_rows, width), f32),
+            dma((4,)),
+            block,
+            block,
+            row_block,
             pltpu.VMEM((BANDS - 1, band, hot_width), f32),
             pltpu.VMEM((2, nx, 2, share, part), f32),
             pltpu.VMEM((n_rep, 8, share), f32),
@@ -185,7 +264,7 @@
         compiler_params=pltpu.CompilerParams(
             collective_id=0, has_side_effects=True, vmem_limit_bytes=40 * 1024 * 1024
         ),
-    )(msg0, msg1, rows, hot)
+    )(messages, lists, numbers, dst, ids, memory, cot, hot_memory, hot_cot)
 
 
 ORDER_A = ("core", "x", "lo", "hi")
@@ -206,7 +285,7 @@
     return [(first, ORDER_B if i % 2 else ORDER_A) for i, first in enumerate(range(0, columns, LANES))]
 
 
-def finish_kernel(n_node, n_rep, g_ref, cold_ref, hot_ref, place_ref, og, ocold, new_hot, *scratch):
+def finish_kernel(n_node, n_rep, hot_base, g_ref, cold_ref, hot_ref, ids_ref, og, ocold, new_hot, *scratch):
     sizes = sizes_of(n_node, n_rep)
     parts = parts_of(g_ref.shape[2])
     send_sem, recv_sem = scratch[:2]
@@ -276,13 +355,14 @@
 
     def hot_start(phase):
         axis = ORDER_HOT[phase]
-        where = ohot.at[pl.ds(prefix(ORDER_HOT, phase), span(sizes, ORDER_HOT, phase))]
+        spot = [mine[a] if a in ORDER_HOT[: phase + 1] else slice(None) for a in ("hi", "lo", "x", "core")]
+        where = ohot.at[tuple(spot)]
         return [ship(where, where, peer(axis, k)) for k in range(1, sizes[axis])]
 
     everyone = range(len(parts))
     flying = [scatter_start(part, 0) for part in everyone]
     ocold[mine["x"], mine["core"]] = cold_ref[...]
-    ohot[prefix(ORDER_HOT, 3)] = hot_ref[...]
+    ohot[mine["hi"], mine["lo"], mine["x"], mine["core"]] = hot_ref[...]
     cold_place = ocold.at[mine["x"], mine["core"]]
     hot_copies = hot_start(3)
     cold_copies = [ship(cold_place, cold_place, peer("x", k)) for k in range(1, sizes["x"])]
@@ -315,7 +395,7 @@
     def permute_hot(part):
         step = new_hot.shape[0] // 4
         chosen = lax.broadcasted_iota(jnp.int32, (new_hot.shape[0], step), 0)
-        chosen = chosen == place_ref[0:1, part * step : (part + 1) * step]
+        chosen = chosen == ids_ref[:, part * step : (part + 1) * step] - hot_base
         got = lax.dot_general(
             jnp.where(chosen, 1.0, 0.0).astype(jnp.bfloat16),
             pieces[...],
@@ -335,7 +415,7 @@
         copy.wait_send()
 
 
-def finish(n_node, n_rep, grads, cold, hot, place):
+def finish(n_node, n_rep, hot_base, grads, cold, hot, ids):
     sizes = sizes_of(n_node, n_rep)
     f32 = jnp.float32
     n_dev, piece, columns = grads.shape
@@ -348,14 +428,14 @@
             block = (span(sizes, order, phase), piece, LANES)
             scratch += [pltpu.VMEM((sizes[order[phase]] - 1, *block), f32), pltpu.VMEM(block, f32)]
     band, width = hot.shape
-    hot_rows = place.shape[1]
-    blocks = (n_dev, band, width)
+    hot_rows = ids.shape[1]
+    blocks = (sizes["hi"], sizes["lo"], sizes["x"], 2, band, width)
     out_hot = jax.ShapeDtypeStruct(blocks, f32)
     if band % 8 == 0:
         out_hot = jax.ShapeDtypeStruct((hot_rows, width), f32)
         scratch += [pltpu.VMEM(blocks, f32), pltpu.VMEM((hot_rows, 3 * width), jnp.bfloat16)]
     return pl.pallas_call(
-        functools.partial(finish_kernel, n_node, n_rep),
+        functools.partial(finish_kernel, n_node, n_rep, hot_base),
         out_shape=(
             jax.ShapeDtypeStruct(grads.shape, f32),
             jax.ShapeDtypeStruct((sizes["x"], 2, *cold.shape), f32),
@@ -367,7 +447,7 @@
         compiler_params=pltpu.CompilerParams(
             collective_id=1, has_side_effects=True, vmem_limit_bytes=40 * 1024 * 1024
         ),
-    )(grads, cold, hot, place)
+    )(grads, cold, hot, ids)
 
 
 def on_device(
@@ -394,14 +474,12 @@
     n_rep = lax.axis_size("rep")
     n_dev = n_node * n_rep
     rows_dev, width = memory.shape
-    slot_cap = cold_list.shape[1]
     hot_rows = hot_memory.shape[0]
     events = src_local.shape[0]
     msg_width = w_msg.shape[1]
     band = hot_rows // n_dev
     share = rows_dev // n_rep
     rep = lax.axis_index("rep")
-    me = lax.axis_index("node") * n_rep + rep
     hot_base = n_node * rows_dev
 
     pick = (src_local[:, None] == jnp.arange(rows_dev, dtype=jnp.int32)[None, :]).astype(bf16)
@@ -410,53 +488,23 @@
     raw = jnp.concatenate([src_mem, edge_feat, enc], axis=1)
     messages = jax.nn.silu(jnp.dot(raw, w_msg, preferred_element_type=f32) + b_msg[None, :]).astype(bf16)
 
-    local_row = lax.rem(dst_ids, rows_dev)
-    lane = jnp.arange(128, dtype=jnp.int32)[None, :]
-    extra = jnp.where(
-        lane == 0, lax.div(local_row, 32)[:, None], jnp.where(lane == 1, lax.rem(local_row, 32)[:, None], 0)
-    ).astype(bf16)
-    hot_place = jnp.where(
-        dst_ids >= hot_base, lax.rem(dst_ids - hot_base + hot_rows - me * band, hot_rows), -1
+    ids_row = hot_ids.reshape(1, hot_rows)
+    cold_total, cold_cnt, hot_sum, mem, cot = exchange(
+        n_node,
+        n_rep,
+        messages,
+        cold_list,
+        cold_count.reshape(n_node, 1),
+        dst_ids.reshape(1, events),
+        ids_row,
+        memory,
+        cot_cold,
+        hot_memory,
+        cot_hot,
     )
-    flat_list = cold_list.reshape(-1)
-    event = jnp.arange(events, dtype=jnp.int32)[None, :]
-    listed = (flat_list[:, None] == event).astype(bf16)
-    hot_match = (jnp.arange(BANDS * band, dtype=jnp.int32)[:, None] == hot_place[None, :]).astype(bf16)
-    part = msg_width // 2
-    msg0, msg1 = (
-        jnp.dot(listed, messages[:, h * part : (h + 1) * part], preferred_element_type=f32)
-        .astype(bf16)
-        .reshape(n_node, slot_cap, part)
-        for h in range(2)
-    )
-    sent = jnp.dot(listed, extra, preferred_element_type=f32)
-    hot_part = jnp.dot(hot_match, messages, preferred_element_type=f32)
-    hot_number = jnp.sum(hot_match.astype(f32), axis=1)
-    hot_part = jnp.concatenate(
-        [hot_part, jnp.broadcast_to(hot_number[:, None], (BANDS * band, 128))], axis=1
-    )
-    slots = jnp.arange(slot_cap, dtype=jnp.int32)
-    valid = slots[None, :] < cold_count[:, None]
-    row_at = (sent[:, 0] * 32.0 + sent[:, 1]).astype(jnp.int32)
-    send_row = jnp.where(valid, row_at.reshape(n_node, slot_cap), -1)
-    send_row = jnp.pad(send_row, ((0, 0), (0, 128 - slot_cap)), constant_values=-1)
-    send_row = jnp.broadcast_to(send_row[:, None, :], (n_node, 8, 128))
-
-    cold_total, cold_cnt, hot_sum = exchange(
-        n_node, n_rep, rows_dev, msg0, msg1, send_row, hot_part.reshape(BANDS, band, msg_width + 128)
-    )
-    first = rep * share
     cold_number = lax.dynamic_index_in_dim(cold_cnt, rep, 0, keepdims=False)[0]
     total = jnp.concatenate([cold_total, hot_sum[:, :msg_width]], axis=0)
     count = jnp.concatenate([cold_number, hot_sum[:, msg_width]], axis=0)
-
-    own_ids = hot_base + me * band + jnp.arange(band, dtype=jnp.int32)
-    own = (own_ids[:, None] == hot_ids[None, :]).astype(f32)
-    hot_state = jnp.dot(
-        own, jnp.concatenate([hot_memory, cot_hot], axis=1), precision=lax.Precision.HIGHEST
-    )
-    mem = jnp.concatenate([lax.dynamic_slice_in_dim(memory, first, share, 0), hot_state[:, :width]], axis=0)
-    cot = jnp.concatenate([lax.dynamic_slice_in_dim(cot_cold, first, share, 0), hot_state[:, width:]], axis=0)
 
     agg = (total / jnp.maximum(count, 1.0)[:, None]).astype(bf16)
     live = (count > 0)[:, None]
@@ -478,26 +526,14 @@
     grad_a = jnp.dot(agg.astype(f32).T, d_input, precision=lax.Precision.HIGHEST)
     grad_b = jnp.dot(mem_wide.T, d_hidden, precision=lax.Precision.HIGHEST)
     grads = jnp.concatenate([grad_a, grad_b], axis=0)
-    sizes = sizes_of(n_node, n_rep)
-    ids = hot_ids - hot_base
-    block, inner = lax.div(ids, band), lax.rem(ids, band)
-    at_node, at_rep = lax.div(block, n_rep), lax.rem(block, n_rep)
-    spot = {
-        "hi": lax.div(at_node, sizes["lo"]),
-        "lo": lax.rem(at_node, sizes["lo"]),
-        "x": lax.div(at_rep, 2),
-        "core": lax.rem(at_rep, 2),
-    }
-    place = sum(spot[a] * span(sizes, ORDER_HOT, i) for i, a in enumerate(ORDER_HOT)) * band + inner
-    place_rows = jnp.broadcast_to(place[None, :], (8, hot_rows))
     g_rows, g_cols = grads.shape
     grads, new_cold, new_hot = finish(
-        n_node, n_rep, grads.reshape(n_dev, g_rows // n_dev, g_cols), fresh[:share], fresh[share:], place_rows
+        n_node, n_rep, hot_base, grads.reshape(n_dev, g_rows // n_dev, g_cols), fresh[:share], fresh[share:], ids_row
     )
     grads = grads.reshape(g_rows, g_cols)
     agg_rows = w_in.shape[0]
     if band % 8:
-        new_hot = jnp.take(new_hot.reshape(hot_rows, width), place, axis=0)
+        new_hot = jnp.take(new_hot.reshape(hot_rows, width), hot_ids - hot_base, axis=0)
     return (new_cold.reshape(rows_dev, width), new_hot, grads[:agg_rows], grads[agg_rows:])
 
 

time: 112 us -> 108 us (0.964)
  matrix products: 10.8 us -> 6.26 us
    dot_general x5 -> x0, matrix products: 5.55 us -> none  [the longest x1 2.44 us: on_device(): jnp.dot(own, jnp.concatenate([hot_memory, cot_hot], axis=1), precision=la...]
    pallas_call x1, Pallas kernels: 42.6 us -> 44.7 us  [exchange(): pl.pallas_call(functools.partial(exchange_kernel, n_node, n_rep), out_sha...]
    unnamed x25 -> x26, local copies, waits for them, and re-layouts: 2.5 us -> 3.1 us
where the time goes in v4:
time: 108 us; the launch traced here: 107 us
  Pallas kernels  89.7 us (83%)
  matrix products  6.26 us (6%)
  local copies, waits for them, and re-layouts  6.15 us (6%)
  other arithmetic  4.29 us (4%)
    pallas_call x1, Pallas kernels, finish(): pl.pallas_call(functools.partial(finish_kernel, n_node, n_rep, hot_base),...  45 us
    pallas_call x1, Pallas kernels, exchange(): pl.pallas_call(functools.partial(exchange_kernel, n_node, n_rep), out_sha...  44.7 us
    unnamed x26, local copies, waits for them, and re-layouts  3.1 us
    convert_element_type x1, other arithmetic, on_device(): jnp.cos(times.astype(f32)[:, None] * time_freq[None, :] + time_phase[None...  2.68 us

profile of v4, /device:TPU:1, one launch (start us, length us, event | category | flops | bytes accessed | tf_op | source)
XLA Modules:
  0.0 107.3 jit_solution(12388579694214363491)
XLA Ops:
  0.6 0.0 copy-start
  0.6 0.0 copy-start.11
  0.7 0.0 copy-start.9
  0.7 0.0 copy-start.10
  0.7 0.8 convert_element_type.26
  1.5 0.7 copy.22.number_ref
  2.2 2.7 %cosine_convert_fusion = bf16[1024,128]{1,0:T(8,128)(2,1)S(1)} fusion(f32[128]{0:T(128)} %param.29, f32[128]{0:T(128)} %param.28, f32[1024]{0:T(1024)S(1)} %convert_element_type.26), kind=kLoop, calls=%fused_computation.20 | loop fusion | flops 393216 | bytes 267264 | tf_op jit(solution)/shard_map/convert_element_type | solution.py:487
  4.9 2.1 %fusion.2 = bf16[1024,256]{1,0:T(8,128)(2,1)S(1)} fusion(s32[1024]{0:T(1024)} %param.21, f32[1024,256]{1,0:T(8,128)} %memory_any.1), kind=kOutput, calls=%fused_computation.5 | convolution fusion | flops 538443776 | bytes 1576960 | tf_op jit(solution)/shard_map/dot_general | solution.py:486
  7.0 0.0 copy-done.11
  7.0 0.0 copy-done.9
  7.0 0.0 copy-done.10
  7.0 0.0 copy-start.1
  7.0 0.0 copy-start.2
  7.0 0.0 copy-start.3
  7.1 0.0 copy-start.4
  7.1 0.0 copy-start.5
  7.1 0.0 copy-start.6
  7.1 0.0 copy-start.7
  7.1 1.0 multiply_convert_fusion.messages_ref
  8.1 0.1 copy-done.1
  8.2 0.3 copy-done.2
  8.6 0.3 copy-done.3
  8.9 0.3 copy-done.4
  9.2 0.0 copy-done.5
  9.2 0.0 copy-done.6
  9.2 0.0 copy-done.7
  9.2 0.0 copy-start.8
  9.2 44.7 %shard_map.192 = (f32[256,512]{1,0:T(8,128)S(1)}, f32[4,8,256]{2,1,0:T(8,128)S(1)}, f32[32,640]{1,0:T(8,128)S(1)}, f32[288,256]{1,0:T(8,128)S(1)}, f32[288,256]{1,0:T(8,128)S(1)}) custom-call(bf16[1024,512]{1,0:T(8,128)(2,1)S(1)} %multiply_convert_fusion.messages_ref, s32[8,128]{1,0:T(8,128)S(1)} %copy-done.6, s32[8,1]{1,0:T(8,128)S(1)} %copy.22.number_ref, ...), custom_call_target="tpu_custom_call" | custom-call | tf_op jit(solution)/shard_map/pallas_call | solution.py:227
  53.9 0.1 slice_reduce_fusion
  54.1 0.0 copy-done.8
  54.1 0.3 fusion.37
  54.4 0.0 copy-done
  54.4 0.4 fusion.33
  54.8 0.2 add_select_fusion
  55.1 0.3 subtract_multiply_fusion
  55.4 0.1 fusion.35
  55.5 0.9 fusion.10
  56.4 1.6 %fusion.8 = f32[512,768]{1,0:T(8,128)S(1)} fusion(f32[288,256]{1,0:T(8,128)S(1)} %get-tuple-element.23, f32[288,256]{1,0:T(8,128)S(1)} %get-tuple-element.24, f32[288,256]{1,0:T(8,128)S(1)} %get-tuple-element.22, f32[32,512]{1,0:T(8,128)S(1)} %slice.40, f32[256,512]{1,0:T(8,128)S(1)} %get-tuple-element.12, f32[288]{0:T(512)S(1)} %fusion.26), kind=kOutput, calls=%fused_computation.12 | convolution fusion | flops 1360060416 | bytes 3048576 | tf_op jit(solution)/shard_map/dot_general | solution.py:526
  58.0 0.2 pad_maximum_fusion
  58.2 45.0 %shard_map.193 = (f32[32,24,768]{2,1,0:T(8,128)S(1)}, f32[2,2,256,256]{3,2,1,0:T(8,128)S(1)}, f32[1024,256]{1,0:T(8,128)S(1)}) custom-call(f32[32,24,768]{2,1,0:T(8,128)S(1)} %bitcast.12, f32[256,256]{1,0:T(8,128)S(1)} %slice.59.cold_ref, f32[32,256]{1,0:T(8,128)S(1)} %slice.60.hot_ref, s32[1,1024]{1,0:T(1,128)S(1)} %bitcast.17), custom_call_target="tpu_custom_call" | custom-call | tf_op jit(solution)/shard_map/pallas_call | solution.py:437
  103.2 0.9 slice.62
  104.1 1.2 %slice.61 = f32[512,768]{1,0:T(8,128)} slice(f32[768,768]{1,0:T(8,128)S(1)} %bitcast.14), slice={[0:512], [0:768]} | slice | bytes 3145728 | tf_op jit(solution)/shard_map/slice | solution.py:537
  105.3 1.0 copy.25
  106.3 1.0 copy.26
  (7 shorter events, 0.1 us)
Async XLA Ops:
  0.6 53.8 %copy-start = (bf16[512,768]{1,0:T(8,128)(2,1)S(1)}, bf16[512,768]{1,0:T(8,128)(2,1)}, u32[]{:S(2)}) copy-start(bf16[512,768]{1,0:T(8,128)(2,1)} %param.32) | copy-start | bytes 2359300
  0.6 6.3 %copy-start.11 = (f32[512]{0:T(512)S(1)}, f32[512]{0:T(512)}, u32[]{:S(2)}) copy-start(f32[512]{0:T(512)} %param.31) | copy-start | bytes 6148
  0.7 6.3 %copy-start.9 = (bf16[512,512]{1,0:T(8,128)(2,1)S(1)}, bf16[512,512]{1,0:T(8,128)(2,1)}, u32[]{:S(2)}) copy-start(bf16[512,512]{1,0:T(8,128)(2,1)} %param.30) | copy-start | bytes 1572868
  0.7 6.3 %copy-start.10 = (bf16[1024,128]{1,0:T(8,128)(2,1)S(1)}, bf16[1024,128]{1,0:T(8,128)(2,1)}, u32[]{:S(2)}) copy-start(bf16[1024,128]{1,0:T(8,128)(2,1)} %param.24) | copy-start | bytes 786436
  7.0 1.2 %copy-start.1 = (f32[1024,256]{1,0:T(8,128)S(1)}, f32[1024,256]{1,0:T(8,128)}, u32[]{:S(2)}) copy-start(f32[1024,256]{1,0:T(8,128)} %memory_any.1) | copy-start | bytes 3145732
  7.0 1.5 %copy-start.2 = (f32[1024,256]{1,0:T(8,128)S(1)}, f32[1024,256]{1,0:T(8,128)}, u32[]{:S(2)}) copy-start(f32[1024,256]{1,0:T(8,128)} %cot_any.1) | copy-start | bytes 3145732
  7.0 1.8 %copy-start.3 = (f32[1024,256]{1,0:T(8,128)S(1)}, f32[1024,256]{1,0:T(8,128)}, u32[]{:S(2)}) copy-start(f32[1024,256]{1,0:T(8,128)} %hot_memory_any.1) | copy-start | bytes 3145732
  7.1 2.1 %copy-start.4 = (f32[1024,256]{1,0:T(8,128)S(1)}, f32[1024,256]{1,0:T(8,128)}, u32[]{:S(2)}) copy-start(f32[1024,256]{1,0:T(8,128)} %hot_cot_any.1) | copy-start | bytes 3145732
  7.1 2.1 %copy-start.5 = (s32[1024]{0:T(1024)S(1)}, s32[1024]{0:T(1024)}, u32[]{:S(2)}) copy-start(s32[1024]{0:T(1024)} %param.27) | copy-start | bytes 12292
  7.1 2.1 %copy-start.6 = (s32[8,128]{1,0:T(8,128)S(1)}, s32[8,128]{1,0:T(8,128)}, u32[]{:S(2)}) copy-start(s32[8,128]{1,0:T(8,128)} %list_ref.1) | copy-start | bytes 12292
  7.1 2.1 %copy-start.7 = (s32[1024]{0:T(1024)S(1)}, s32[1024]{0:T(1024)}, u32[]{:S(2)}) copy-start(s32[1024]{0:T(1024)} %param.22) | copy-start | bytes 12292
  9.2 44.9 %copy-start.8 = (bf16[256,768]{1,0:T(8,128)(2,1)S(1)}, bf16[256,768]{1,0:T(8,128)(2,1)}, u32[]{:S(2)}) copy-start(bf16[256,768]{1,0:T(8,128)(2,1)} %param.33) | copy-start | bytes 1179652

commit v5 on v4

--- a/solution.py
+++ b/solution.py
@@ -33,9 +33,10 @@
     n_node, n_rep,
     messages_ref, list_ref, number_ref, dst_ref, ids_ref, memory_any, cot_any, hot_memory_any, hot_cot_any,
     sum_out, cnt_out, hot_out, mem_out, cot_out,
-    msg0_ref, msg1_ref, rows_ref, hot_ref, hot_state, own_sem,
-    recv0, recv1, rows_recv, hot_recv, sums, cnts, core_recv, x_send, x_recv, cnt_core, cnt_send, cnt_x,
+    rows_ref, hot_ref, hot_state, own_sem,
+    rows_recv, hot_recv, cnts, cnt_core, cnt_send, cnt_x,
     msg_s, msg_r, row_s, row_r, hot_s, hot_r, core_s, core_r, x_s, x_r, cc_s, cc_r, cx_s, cx_r,
+    *chunked,
 ):
     nx = n_rep // 2
     n_dev = n_node * n_rep
@@ -44,7 +45,12 @@
     core = lax.rem(rep, 2)
     xi = lax.div(rep, 2)
     me = node * n_rep + rep
-    cap, part = msg0_ref.shape[1:]
+    cap = list_ref.shape[1]
+    msg_width = messages_ref.shape[1]
+    cuts = cuts_of(msg_width)
+    msg_refs, recvs, sums, core_recv, x_send, x_recv = (
+        chunked[i * len(cuts) : (i + 1) * len(cuts)] for i in range(6)
+    )
     share = sum_out.shape[0]
     rows_dev = share * n_rep
     events = messages_ref.shape[0]
@@ -105,8 +111,8 @@
         block = lax.dot_general(
             listed, messages_ref[...], (((0,), (0,)), ((), ())), preferred_element_type=f32
         ).astype(bf16)
-        msg0_ref[other] = block[:, :part]
-        msg1_ref[other] = block[:, part:]
+        for ref, (begin, size) in zip(msg_refs, cuts):
+            ref[other] = block[:, begin : begin + size]
         found = jnp.dot(digits, listed, preferred_element_type=f32)
         row = (found[0:1] * 32.0 + found[1:2]).astype(jnp.int32)
         row = jnp.where(slot < number_ref[pl.ds(other, 1), :], row, -1)
@@ -117,10 +123,15 @@
         other = node_at(a, b)
         build(other)
         arrivals["row", k] = push(rows_ref.at[other], rows_recv.at[node], row_s.at[k], row_r.at[k], (other, rep))
-        arrivals[0, k] = push(msg0_ref.at[other], recv0.at[node], msg_s.at[0, k], msg_r.at[0, k], (other, rep))
-    for k, (a, b) in enumerate(steps):
-        other = node_at(a, b)
-        arrivals[1, k] = push(msg1_ref.at[other], recv1.at[node], msg_s.at[1, k], msg_r.at[1, k], (other, rep))
+        arrivals[0, k] = push(
+            msg_refs[0].at[other], recvs[0].at[node], msg_s.at[0, k], msg_r.at[0, k], (other, rep)
+        )
+    for h in range(1, len(cuts)):
+        for k, (a, b) in enumerate(steps):
+            other = node_at(a, b)
+            arrivals[h, k] = push(
+                msg_refs[h].at[other], recvs[h].at[node], msg_s.at[h, k], msg_r.at[h, k], (other, rep)
+            )
     sent = list(arrivals.values())
 
     place = dst - hot_base - me * band
@@ -130,8 +141,8 @@
     hot_part = jnp.dot(match.astype(bf16), messages_ref[...], preferred_element_type=f32)
     hot_number = jnp.sum(match, axis=1, keepdims=True)
     for j in range(BANDS):
-        hot_ref[j, :, : 2 * part] = hot_part[j * band : (j + 1) * band]
-        hot_ref[j, :, 2 * part :] = jnp.broadcast_to(hot_number[j * band : (j + 1) * band], (band, 128))
+        hot_ref[j, :, :msg_width] = hot_part[j * band : (j + 1) * band]
+        hot_ref[j, :, msg_width:] = jnp.broadcast_to(hot_number[j * band : (j + 1) * band], (band, 128))
     hots = [
         push(hot_ref.at[j], hot_recv.at[j - 1], hot_s.at[j - 1], hot_r.at[j - 1], at_linear(j))
         for j in range(1, BANDS)
@@ -147,7 +158,8 @@
         rows = jnp.dot(own, hot_state[i], precision=lax.Precision.HIGHEST, preferred_element_type=f32)
         out[share : share + band] = rows[:band]
 
-    sums[...] = jnp.zeros_like(sums)
+    for ref in sums:
+        ref[...] = jnp.zeros_like(ref)
     cnts[...] = jnp.zeros_like(cnts)
     ones = jnp.ones((8, cap), jnp.bfloat16)
 
@@ -155,15 +167,15 @@
         for s in range(n_rep):
             spot = lax.broadcasted_iota(jnp.int32, (share, cap), 0) + s * share
             equal = jnp.where(spot == rows, 1.0, 0.0).astype(jnp.bfloat16)
-            sums[h, s // 2, s % 2] += jnp.dot(equal, block, preferred_element_type=jnp.float32)
+            sums[h][s // 2, s % 2] += jnp.dot(equal, block, preferred_element_type=jnp.float32)
             if h == 0:
                 cnts[s] += lax.dot_general(
                     ones, equal, (((1,), (1,)), ((), ())), preferred_element_type=jnp.float32
                 )
 
-    crossing = [[], []]
+    crossing = [[] for _ in cuts]
     counts = []
-    for h, (mine, got) in enumerate(((msg0_ref, recv0), (msg1_ref, recv1))):
+    for h, (mine, got) in enumerate(zip(msg_refs, recvs)):
         add_block(h, rows_ref[node, 0:1, :cap], mine[node])
         for k, (a, b) in enumerate(steps):
             if h == 0:
@@ -174,7 +186,7 @@
         halves = []
         for k in [*range(1, nx), 0]:
             p = lax.rem(xi + k, nx)
-            copy = push(sums.at[h, p, 1 - core], core_recv.at[h, k], core_s.at[h, k], core_r.at[h, k], other_core)
+            copy = push(sums[h].at[p, 1 - core], core_recv[h].at[k], core_s.at[h, k], core_r.at[h, k], other_core)
             halves.append((k, p, copy))
         if h == 0:
             cnt_copy = push(cnts, cnt_core, cc_s, cc_r, other_core)
@@ -183,9 +195,9 @@
             copy.wait_recv()
             sent.append(copy)
             if k:
-                x_send[h, k - 1] = sums[h, p, core] + core_recv[h, k]
+                x_send[h][k - 1] = sums[h][p, core] + core_recv[h][k]
                 crossing[h].append(
-                    push(x_send.at[h, k - 1], x_recv.at[h, k - 1], x_s.at[h, k - 1], x_r.at[h, k - 1], at_x(k))
+                    push(x_send[h].at[k - 1], x_recv[h].at[k - 1], x_s.at[h, k - 1], x_r.at[h, k - 1], at_x(k))
                 )
         if h == 0:
             cnt_copy.wait_recv()
@@ -201,33 +213,41 @@
         copy.wait_recv()
         number += cnt_x[k]
     cnt_out[...] = number
-    for h in range(2):
-        total = sums[h, xi, core] + core_recv[h, 0]
+    for h, (begin, size) in enumerate(cuts):
+        total = sums[h][xi, core] + core_recv[h][0]
         for k, copy in enumerate(crossing[h]):
             copy.wait_recv()
-            total += x_recv[h, k]
-        sum_out[:, h * part : (h + 1) * part] = total
-    for copy in [*sent, *crossing[0], *crossing[1], *counts]:
+            total += x_recv[h][k]
+        sum_out[:, begin : begin + size] = total
+    for copy in [*sent, *sum(crossing, []), *counts]:
         copy.wait_send()
+
+
+def cuts_of(width):
+    return [(0, width // 2), (width // 2, width // 4), (3 * width // 4, width // 4)]
 
 
 def exchange(n_node, n_rep, messages, lists, numbers, dst, ids, memory, cot, hot_memory, hot_cot):
     nx = n_rep // 2
     cap = lists.shape[1]
-    part = messages.shape[1] // 2
+    msg_width = messages.shape[1]
+    cuts = cuts_of(msg_width)
     rows_dev, width = memory.shape
     hot_rows = hot_memory.shape[0]
     band = hot_rows // (n_node * n_rep)
-    hot_width = 2 * part + 128
+    hot_width = msg_width + 128
     share = rows_dev // n_rep
     dma = pltpu.SemaphoreType.DMA
     f32 = jnp.float32
-    block = pltpu.VMEM((n_node, cap, part), messages.dtype)
+
+    def chunked(*shape, dtype=jnp.float32):
+        return [pltpu.VMEM((*shape, size), dtype) for _, size in cuts]
+
     row_block = pltpu.VMEM((n_node, 8, 128), jnp.int32)
     return pl.pallas_call(
         functools.partial(exchange_kernel, n_node, n_rep),
         out_shape=(
-            jax.ShapeDtypeStruct((share, 2 * part), f32),
+            jax.ShapeDtypeStruct((share, msg_width), f32),
             jax.ShapeDtypeStruct((n_rep, 8, share), f32),
             jax.ShapeDtypeStruct((band, hot_width), f32),
             jax.ShapeDtypeStruct((share + band, width), f32),
@@ -236,30 +256,28 @@
         in_specs=[VMEM] * 5 + [pl.BlockSpec(memory_space=pl.ANY)] * 4,
         out_specs=(VMEM,) * 5,
         scratch_shapes=[
-            block,
-            block,
             row_block,
             pltpu.VMEM((BANDS, band, hot_width), f32),
             pltpu.VMEM((2, hot_rows, width), f32),
             dma((4,)),
-            block,
-            block,
             row_block,
             pltpu.VMEM((BANDS - 1, band, hot_width), f32),
-            pltpu.VMEM((2, nx, 2, share, part), f32),
             pltpu.VMEM((n_rep, 8, share), f32),
-            pltpu.VMEM((2, nx, share, part), f32),
-            pltpu.VMEM((2, nx - 1, share, part), f32),
-            pltpu.VMEM((2, nx - 1, share, part), f32),
             pltpu.VMEM((n_rep, 8, share), f32),
             pltpu.VMEM((n_rep, 8, share), f32),
             pltpu.VMEM((nx - 1, n_rep, 8, share), f32),
-            dma((2, n_node)), dma((2, n_node)), dma((n_node,)), dma((n_node,)),
+            dma((len(cuts), n_node)), dma((len(cuts), n_node)), dma((n_node,)), dma((n_node,)),
             dma((BANDS - 1,)), dma((BANDS - 1,)),
-            dma((2, nx)), dma((2, nx)),
-            dma((2, nx - 1)), dma((2, nx - 1)),
+            dma((len(cuts), nx)), dma((len(cuts), nx)),
+            dma((len(cuts), nx - 1)), dma((len(cuts), nx - 1)),
             dma, dma,
             dma((nx - 1,)), dma((nx - 1,)),
+            *chunked(n_node, cap, dtype=messages.dtype),
+            *chunked(n_node, cap, dtype=messages.dtype),
+            *chunked(nx, 2, share),
+            *chunked(nx, share),
+            *chunked(nx - 1, share),
+            *chunked(nx - 1, share),
         ],
         compiler_params=pltpu.CompilerParams(
             collective_id=0, has_side_effects=True, vmem_limit_bytes=40 * 1024 * 1024

time: 108 us -> 108 us (level)
    pallas_call x1, Pallas kernels: 45 us -> 46.8 us  [finish(): pl.pallas_call(functools.partial(finish_kernel, n_node, n_rep, hot_base),...]
    pallas_call x1, Pallas kernels: 44.7 us -> 43.1 us  [exchange(): pl.pallas_call(functools.partial(exchange_kernel, n_node, n_rep), out_sha...]
where the time goes in v5:
time: 108 us; the launch traced here: 107 us
  Pallas kernels  89.9 us (83%)
  matrix products  6.26 us (6%)
  local copies, waits for them, and re-layouts  6.15 us (6%)
  other arithmetic  4.29 us (4%)
    pallas_call x1, Pallas kernels, finish(): pl.pallas_call(functools.partial(finish_kernel, n_node, n_rep, hot_base),...  46.8 us
    pallas_call x1, Pallas kernels, exchange(): pl.pallas_call(functools.partial(exchange_kernel, n_node, n_rep), out_sha...  43.1 us
    unnamed x26, local copies, waits for them, and re-layouts  3.1 us
    convert_element_type x1, other arithmetic, on_device(): jnp.cos(times.astype(f32)[:, None] * time_freq[None, :] + time_phase[None...  2.68 us

profile of v5, /device:TPU:1, one launch (start us, length us, event | category | flops | bytes accessed | tf_op | source)
XLA Modules:
  0.0 107.5 jit_solution(4023492776075720096)
XLA Ops:
  0.6 0.0 copy-start
  0.6 0.0 copy-start.11
  0.7 0.0 copy-start.9
  0.7 0.0 copy-start.10
  0.7 0.8 convert_element_type.26
  1.5 0.7 copy.22.number_ref
  2.2 2.7 %cosine_convert_fusion = bf16[1024,128]{1,0:T(8,128)(2,1)S(1)} fusion(f32[128]{0:T(128)} %param.29, f32[128]{0:T(128)} %param.28, f32[1024]{0:T(1024)S(1)} %convert_element_type.26), kind=kLoop, calls=%fused_computation.20 | loop fusion | flops 393216 | bytes 267264 | tf_op jit(solution)/shard_map/convert_element_type | solution.py:505
  4.9 2.1 %fusion.2 = bf16[1024,256]{1,0:T(8,128)(2,1)S(1)} fusion(s32[1024]{0:T(1024)} %param.21, f32[1024,256]{1,0:T(8,128)} %memory_any.1), kind=kOutput, calls=%fused_computation.5 | convolution fusion | flops 538443776 | bytes 1576960 | tf_op jit(solution)/shard_map/dot_general | solution.py:504
  7.0 0.0 copy-done.11
  7.0 0.0 copy-done.9
  7.0 0.0 copy-done.10
  7.0 0.0 copy-start.1
  7.0 0.0 copy-start.2
  7.0 0.0 copy-start.3
  7.1 0.0 copy-start.4
  7.1 0.0 copy-start.5
  7.1 0.0 copy-start.6
  7.1 0.0 copy-start.7
  7.1 1.0 multiply_convert_fusion.messages_ref
  8.1 0.1 copy-done.1
  8.2 0.3 copy-done.2
  8.6 0.3 copy-done.3
  8.9 0.3 copy-done.4
  9.2 0.0 copy-done.5
  9.2 0.0 copy-done.6
  9.2 0.0 copy-done.7
  9.2 0.0 copy-start.8
  9.2 43.1 %shard_map.192 = (f32[256,512]{1,0:T(8,128)S(1)}, f32[4,8,256]{2,1,0:T(8,128)S(1)}, f32[32,640]{1,0:T(8,128)S(1)}, f32[288,256]{1,0:T(8,128)S(1)}, f32[288,256]{1,0:T(8,128)S(1)}) custom-call(bf16[1024,512]{1,0:T(8,128)(2,1)S(1)} %multiply_convert_fusion.messages_ref, s32[8,128]{1,0:T(8,128)S(1)} %copy-done.6, s32[8,1]{1,0:T(8,128)S(1)} %copy.22.number_ref, ...), custom_call_target="tpu_custom_call" | custom-call | tf_op jit(solution)/shard_map/pallas_call | solution.py:247
  52.3 0.1 slice_reduce_fusion
  52.5 0.0 copy-done.8
  52.5 0.3 fusion.37
  52.8 0.0 copy-done
  52.8 0.4 fusion.33
  53.3 0.2 add_select_fusion
  53.5 0.3 subtract_multiply_fusion
  53.8 0.1 fusion.35
  53.9 0.9 fusion.10
  54.8 1.6 %fusion.8 = f32[512,768]{1,0:T(8,128)S(1)} fusion(f32[288,256]{1,0:T(8,128)S(1)} %get-tuple-element.23, f32[288,256]{1,0:T(8,128)S(1)} %get-tuple-element.24, f32[288,256]{1,0:T(8,128)S(1)} %get-tuple-element.22, f32[32,512]{1,0:T(8,128)S(1)} %slice.40, f32[256,512]{1,0:T(8,128)S(1)} %get-tuple-element.12, f32[288]{0:T(512)S(1)} %fusion.26), kind=kOutput, calls=%fused_computation.12 | convolution fusion | flops 1360060416 | bytes 3048576 | tf_op jit(solution)/shard_map/dot_general | solution.py:544
  56.4 0.2 pad_maximum_fusion
  56.6 46.8 %shard_map.193 = (f32[32,24,768]{2,1,0:T(8,128)S(1)}, f32[2,2,256,256]{3,2,1,0:T(8,128)S(1)}, f32[1024,256]{1,0:T(8,128)S(1)}) custom-call(f32[32,24,768]{2,1,0:T(8,128)S(1)} %bitcast.12, f32[256,256]{1,0:T(8,128)S(1)} %slice.59.cold_ref, f32[32,256]{1,0:T(8,128)S(1)} %slice.60.hot_ref, s32[1,1024]{1,0:T(1,128)S(1)} %bitcast.17), custom_call_target="tpu_custom_call" | custom-call | tf_op jit(solution)/shard_map/pallas_call | solution.py:455
  103.4 0.9 slice.62
  104.3 1.2 %slice.61 = f32[512,768]{1,0:T(8,128)} slice(f32[768,768]{1,0:T(8,128)S(1)} %bitcast.14), slice={[0:512], [0:768]} | slice | bytes 3145728 | tf_op jit(solution)/shard_map/slice | solution.py:555
  105.5 1.0 copy.25
  106.5 1.0 copy.26
  (7 shorter events, 0.1 us)
Async XLA Ops:
  0.6 52.2 %copy-start = (bf16[512,768]{1,0:T(8,128)(2,1)S(1)}, bf16[512,768]{1,0:T(8,128)(2,1)}, u32[]{:S(2)}) copy-start(bf16[512,768]{1,0:T(8,128)(2,1)} %param.32) | copy-start | bytes 2359300
  0.6 6.3 %copy-start.11 = (f32[512]{0:T(512)S(1)}, f32[512]{0:T(512)}, u32[]{:S(2)}) copy-start(f32[512]{0:T(512)} %param.31) | copy-start | bytes 6148
  0.7 6.3 %copy-start.9 = (bf16[512,512]{1,0:T(8,128)(2,1)S(1)}, bf16[512,512]{1,0:T(8,128)(2,1)}, u32[]{:S(2)}) copy-start(bf16[512,512]{1,0:T(8,128)(2,1)} %param.30) | copy-start | bytes 1572868
  0.7 6.3 %copy-start.10 = (bf16[1024,128]{1,0:T(8,128)(2,1)S(1)}, bf16[1024,128]{1,0:T(8,128)(2,1)}, u32[]{:S(2)}) copy-start(bf16[1024,128]{1,0:T(8,128)(2,1)} %param.24) | copy-start | bytes 786436
  7.0 1.2 %copy-start.1 = (f32[1024,256]{1,0:T(8,128)S(1)}, f32[1024,256]{1,0:T(8,128)}, u32[]{:S(2)}) copy-start(f32[1024,256]{1,0:T(8,128)} %memory_any.1) | copy-start | bytes 3145732
  7.0 1.5 %copy-start.2 = (f32[1024,256]{1,0:T(8,128)S(1)}, f32[1024,256]{1,0:T(8,128)}, u32[]{:S(2)}) copy-start(f32[1024,256]{1,0:T(8,128)} %cot_any.1) | copy-start | bytes 3145732
  7.0 1.8 %copy-start.3 = (f32[1024,256]{1,0:T(8,128)S(1)}, f32[1024,256]{1,0:T(8,128)}, u32[]{:S(2)}) copy-start(f32[1024,256]{1,0:T(8,128)} %hot_memory_any.1) | copy-start | bytes 3145732
  7.1 2.1 %copy-start.4 = (f32[1024,256]{1,0:T(8,128)S(1)}, f32[1024,256]{1,0:T(8,128)}, u32[]{:S(2)}) copy-start(f32[1024,256]{1,0:T(8,128)} %hot_cot_any.1) | copy-start | bytes 3145732
  7.1 2.1 %copy-start.5 = (s32[1024]{0:T(1024)S(1)}, s32[1024]{0:T(1024)}, u32[]{:S(2)}) copy-start(s32[1024]{0:T(1024)} %param.27) | copy-start | bytes 12292
  7.1 2.1 %copy-start.6 = (s32[8,128]{1,0:T(8,128)S(1)}, s32[8,128]{1,0:T(8,128)}, u32[]{:S(2)}) copy-start(s32[8,128]{1,0:T(8,128)} %list_ref.1) | copy-start | bytes 12292
  7.1 2.1 %copy-start.7 = (s32[1024]{0:T(1024)S(1)}, s32[1024]{0:T(1024)}, u32[]{:S(2)}) copy-start(s32[1024]{0:T(1024)} %param.22) | copy-start | bytes 12292
  9.2 43.3 %copy-start.8 = (bf16[256,768]{1,0:T(8,128)(2,1)S(1)}, bf16[256,768]{1,0:T(8,128)(2,1)}, u32[]{:S(2)}) copy-start(bf16[256,768]{1,0:T(8,128)(2,1)} %param.33) | copy-start | bytes 1179652

commit v6 on v5

--- a/solution.py
+++ b/solution.py
@@ -115,7 +115,9 @@
             ref[other] = block[:, begin : begin + size]
         found = jnp.dot(digits, listed, preferred_element_type=f32)
         row = (found[0:1] * 32.0 + found[1:2]).astype(jnp.int32)
-        row = jnp.where(slot < number_ref[pl.ds(other, 1), :], row, -1)
+        mark = lax.broadcasted_iota(jnp.int32, (1, n_node), 1) == other
+        number = jnp.sum(jnp.where(mark, number_ref[...], 0).astype(f32), axis=1, keepdims=True)
+        row = jnp.where(slot.astype(f32) < number, row, -1)
         rows_ref[other, :, :cap] = jnp.broadcast_to(row, (8, cap))
 
     arrivals = {}
@@ -512,7 +514,7 @@
         n_rep,
         messages,
         cold_list,
-        cold_count.reshape(n_node, 1),
+        cold_count.reshape(1, n_node),
         dst_ids.reshape(1, events),
         ids_row,
         memory,

time: 108 us -> 108 us (level)
    unnamed x26 -> x28, local copies, waits for them, and re-layouts: 3.1 us -> 3.09 us
where the time goes in v6:
time: 108 us; the launch traced here: 107 us
  Pallas kernels  90.4 us (84%)
  matrix products  6.26 us (6%)
  local copies, waits for them, and re-layouts  5.42 us (5%)
  other arithmetic  4.29 us (4%)
    pallas_call x1, Pallas kernels, finish(): pl.pallas_call(functools.partial(finish_kernel, n_node, n_rep, hot_base),...  47.3 us
    pallas_call x1, Pallas kernels, exchange(): pl.pallas_call(functools.partial(exchange_kernel, n_node, n_rep), out_sha...  43.1 us
    unnamed x28, local copies, waits for them, and re-layouts  3.09 us
    convert_element_type x1, other arithmetic, on_device(): jnp.cos(times.astype(f32)[:, None] * time_freq[None, :] + time_phase[None...  2.68 us

profile of v6, /device:TPU:1, one launch (start us, length us, event | category | flops | bytes accessed | tf_op | source)
XLA Modules:
  0.0 107.3 jit_solution(7703401051356687484)
XLA Ops:
  0.6 0.0 copy-start
  0.6 0.0 copy-start.12
  0.7 0.0 copy-start.10
  0.7 0.0 copy-start.11
  0.7 0.8 convert_element_type.26
  1.5 2.7 %cosine_convert_fusion = bf16[1024,128]{1,0:T(8,128)(2,1)S(1)} fusion(f32[128]{0:T(128)} %param.29, f32[128]{0:T(128)} %param.28, f32[1024]{0:T(1024)S(1)} %convert_element_type.26), kind=kLoop, calls=%fused_computation.20 | loop fusion | flops 393216 | bytes 267264 | tf_op jit(solution)/shard_map/convert_element_type | solution.py:507
  4.2 2.1 %fusion.2 = bf16[1024,256]{1,0:T(8,128)(2,1)S(1)} fusion(s32[1024]{0:T(1024)} %param.21, f32[1024,256]{1,0:T(8,128)} %memory_any.1), kind=kOutput, calls=%fused_computation.5 | convolution fusion | flops 538443776 | bytes 1576960 | tf_op jit(solution)/shard_map/dot_general | solution.py:506
  6.3 0.0 copy-done.12
  6.3 0.0 copy-done.10
  6.3 0.0 copy-done.11
  6.3 0.0 copy-start.1
  6.3 0.0 copy-start.2
  6.3 0.0 copy-start.3
  6.3 0.0 copy-start.4
  6.3 0.0 copy-start.5
  6.4 0.0 copy-start.6
  6.4 0.0 copy-start.7
  6.4 0.0 copy-start.8
  6.4 1.0 multiply_convert_fusion.messages_ref
  7.4 0.1 copy-done.1
  7.5 0.3 copy-done.2
  7.8 0.3 copy-done.3
  8.2 0.3 copy-done.4
  8.5 0.0 copy-done.5
  8.5 0.0 copy-done.6
  8.5 0.0 copy-done.7
  8.5 0.0 copy-done.8
  8.5 0.0 copy-start.9
  8.5 43.1 %shard_map.192 = (f32[256,512]{1,0:T(8,128)S(1)}, f32[4,8,256]{2,1,0:T(8,128)S(1)}, f32[32,640]{1,0:T(8,128)S(1)}, f32[288,256]{1,0:T(8,128)S(1)}, f32[288,256]{1,0:T(8,128)S(1)}) custom-call(bf16[1024,512]{1,0:T(8,128)(2,1)S(1)} %multiply_convert_fusion.messages_ref, s32[8,128]{1,0:T(8,128)S(1)} %copy-done.6, s32[1,8]{1,0:T(1,128)S(1)} %bitcast.19, ...), custom_call_target="tpu_custom_call" | custom-call | tf_op jit(solution)/shard_map/pallas_call | solution.py:249
  51.6 0.1 slice_reduce_fusion
  51.8 0.0 copy-done.9
  51.8 0.3 fusion.37
  52.1 0.0 copy-done
  52.1 0.4 fusion.33
  52.5 0.2 add_select_fusion
  52.8 0.3 subtract_multiply_fusion
  53.0 0.1 fusion.35
  53.2 0.9 fusion.10
  54.1 1.6 %fusion.8 = f32[512,768]{1,0:T(8,128)S(1)} fusion(f32[288,256]{1,0:T(8,128)S(1)} %get-tuple-element.23, f32[288,256]{1,0:T(8,128)S(1)} %get-tuple-element.24, f32[288,256]{1,0:T(8,128)S(1)} %get-tuple-element.22, f32[32,512]{1,0:T(8,128)S(1)} %slice.40, f32[256,512]{1,0:T(8,128)S(1)} %get-tuple-element.12, f32[288]{0:T(512)S(1)} %fusion.26), kind=kOutput, calls=%fused_computation.12 | convolution fusion | flops 1360060416 | bytes 3048576 | tf_op jit(solution)/shard_map/dot_general | solution.py:546
  55.7 0.2 pad_maximum_fusion
  55.8 47.3 %shard_map.193 = (f32[32,24,768]{2,1,0:T(8,128)S(1)}, f32[2,2,256,256]{3,2,1,0:T(8,128)S(1)}, f32[1024,256]{1,0:T(8,128)S(1)}) custom-call(f32[32,24,768]{2,1,0:T(8,128)S(1)} %bitcast.12, f32[256,256]{1,0:T(8,128)S(1)} %slice.59.cold_ref, f32[32,256]{1,0:T(8,128)S(1)} %slice.60.hot_ref, s32[1,1024]{1,0:T(1,128)S(1)} %bitcast.17), custom_call_target="tpu_custom_call" | custom-call | tf_op jit(solution)/shard_map/pallas_call | solution.py:457
  103.2 0.9 slice.62
  104.1 1.2 %slice.61 = f32[512,768]{1,0:T(8,128)} slice(f32[768,768]{1,0:T(8,128)S(1)} %bitcast.14), slice={[0:512], [0:768]} | slice | bytes 3145728 | tf_op jit(solution)/shard_map/slice | solution.py:557
  105.4 1.0 copy.23
  106.3 1.0 copy.24
  (7 shorter events, 0.1 us)
Async XLA Ops:
  0.6 51.4 %copy-start = (bf16[512,768]{1,0:T(8,128)(2,1)S(1)}, bf16[512,768]{1,0:T(8,128)(2,1)}, u32[]{:S(2)}) copy-start(bf16[512,768]{1,0:T(8,128)(2,1)} %param.32) | copy-start | bytes 2359300
  0.6 5.6 %copy-start.12 = (f32[512]{0:T(512)S(1)}, f32[512]{0:T(512)}, u32[]{:S(2)}) copy-start(f32[512]{0:T(512)} %param.31) | copy-start | bytes 6148
  0.7 5.6 %copy-start.10 = (bf16[512,512]{1,0:T(8,128)(2,1)S(1)}, bf16[512,512]{1,0:T(8,128)(2,1)}, u32[]{:S(2)}) copy-start(bf16[512,512]{1,0:T(8,128)(2,1)} %param.30) | copy-start | bytes 1572868
  0.7 5.6 %copy-start.11 = (bf16[1024,128]{1,0:T(8,128)(2,1)S(1)}, bf16[1024,128]{1,0:T(8,128)(2,1)}, u32[]{:S(2)}) copy-start(bf16[1024,128]{1,0:T(8,128)(2,1)} %param.24) | copy-start | bytes 786436
  6.3 1.2 %copy-start.1 = (f32[1024,256]{1,0:T(8,128)S(1)}, f32[1024,256]{1,0:T(8,128)}, u32[]{:S(2)}) copy-start(f32[1024,256]{1,0:T(8,128)} %memory_any.1) | copy-start | bytes 3145732
  6.3 1.5 %copy-start.2 = (f32[1024,256]{1,0:T(8,128)S(1)}, f32[1024,256]{1,0:T(8,128)}, u32[]{:S(2)}) copy-start(f32[1024,256]{1,0:T(8,128)} %cot_any.1) | copy-start | bytes 3145732
  6.3 1.8 %copy-start.3 = (f32[1024,256]{1,0:T(8,128)S(1)}, f32[1024,256]{1,0:T(8,128)}, u32[]{:S(2)}) copy-start(f32[1024,256]{1,0:T(8,128)} %hot_memory_any.1) | copy-start | bytes 3145732
  6.3 2.1 %copy-start.4 = (f32[1024,256]{1,0:T(8,128)S(1)}, f32[1024,256]{1,0:T(8,128)}, u32[]{:S(2)}) copy-start(f32[1024,256]{1,0:T(8,128)} %hot_cot_any.1) | copy-start | bytes 3145732
  6.3 2.1 %copy-start.5 = (s32[1024]{0:T(1024)S(1)}, s32[1024]{0:T(1024)}, u32[]{:S(2)}) copy-start(s32[1024]{0:T(1024)} %param.27) | copy-start | bytes 12292
  6.4 2.1 %copy-start.6 = (s32[8,128]{1,0:T(8,128)S(1)}, s32[8,128]{1,0:T(8,128)}, u32[]{:S(2)}) copy-start(s32[8,128]{1,0:T(8,128)} %list_ref.1) | copy-start | bytes 12292
  6.4 2.1 %copy-start.7 = (s32[1024]{0:T(1024)S(1)}, s32[1024]{0:T(1024)}, u32[]{:S(2)}) copy-start(s32[1024]{0:T(1024)} %param.22) | copy-start | bytes 12292
  6.4 2.1 %copy-start.8 = (s32[8]{0:T(128)S(1)}, s32[8]{0:T(128)}, u32[]{:S(2)}) copy-start(s32[8]{0:T(128)} %param.26) | copy-start | bytes 100
  8.5 43.3 %copy-start.9 = (bf16[256,768]{1,0:T(8,128)(2,1)S(1)}, bf16[256,768]{1,0:T(8,128)(2,1)}, u32[]{:S(2)}) copy-start(bf16[256,768]{1,0:T(8,128)(2,1)} %param.33) | copy-start | bytes 1179652
